TPU v7x, 256 devices: a whole 4x4x8 slice. The times are simulated.
256 devices in a mesh: mode: 8 (over x, y_lo), space: 32 (over y_hi, z, core).
Axes of the slice: x: 4, y: 4 (y_hi: 2, y_lo: 2; y = y_hi * 2 + y_lo), z: 8, core: 2. Of those that a mesh axis runs over, the one named last changes fastest.
Arguments:
- basis: float32 [192, 3, 64, 16, 128], P('mode', None, 'space'), may hold values from -6 to 6
- density: float32 [64, 16, 128], P('space'), may hold values from 0.03 to 1
Outputs:
- rotated: float32 [192, 3, 64, 16, 128], P('mode', None, 'space')
- reduced: float32 [192, 192], replicated
All inputs are finite; a program needn't handle non-finite values.
Results may differ from a plain program's by a relative error of at most 0.00011.
Values sent between devices are 32-bit elements; how exact they have to be, the bound alone decides.
No kernel may reach another device: no remote copies, remote signals or barrier semaphores. Data moves between devices by JAX's collectives and lax.ppermute only.
A program may use at most 128 MiB of HBM per device.

v0:
```python
import functools
import math

import jax
import jax.numpy as jnp
import numpy as np
from jax import lax
from jax.experimental import pallas as pl
from jax.experimental.pallas import tpu as pltpu
from jax.sharding import Mesh, PartitionSpec as P

VMEM = pltpu.VMEM
MODE = ("x", "yl")
SPACE = ("yh", "zc")
F32 = jnp.float32
BF16 = jnp.bfloat16


def hex_matrices():
    poisson = 0.3
    lame_first = poisson / ((1.0 + poisson) * (1.0 - 2.0 * poisson))
    shear = 1.0 / (2.0 * (1.0 + poisson))
    elastic = np.zeros((6, 6))
    elastic[:3, :3] = lame_first
    for number in range(3):
        elastic[number, number] += 2.0 * shear
        elastic[number + 3, number + 3] = shear
    points = [0.5 - 0.5 / math.sqrt(3.0), 0.5 + 0.5 / math.sqrt(3.0)]
    corners = [(a, b, c) for a in (0, 1) for b in (0, 1) for c in (0, 1)]
    stiff = np.zeros((24, 24))
    for point_x in points:
        for point_y in points:
            for point_z in points:
                strain = np.zeros((6, 24))
                for number, corner in enumerate(corners):
                    shape_x = point_x if corner[0] else 1.0 - point_x
                    shape_y = point_y if corner[1] else 1.0 - point_y
                    shape_z = point_z if corner[2] else 1.0 - point_z
                    deriv_x = (2.0 * corner[0] - 1.0) * shape_y * shape_z
                    deriv_y = shape_x * (2.0 * corner[1] - 1.0) * shape_z
                    deriv_z = shape_x * shape_y * (2.0 * corner[2] - 1.0)
                    strain[0, 3 * number] = deriv_x
                    strain[1, 3 * number + 1] = deriv_y
                    strain[2, 3 * number + 2] = deriv_z
                    strain[3, 3 * number] = deriv_y
                    strain[3, 3 * number + 1] = deriv_x
                    strain[4, 3 * number + 1] = deriv_z
                    strain[4, 3 * number + 2] = deriv_y
                    strain[5, 3 * number] = deriv_z
                    strain[5, 3 * number + 2] = deriv_x
                stiff += strain.T @ elastic @ strain / 8.0
    line = np.array([[1.0 / 3.0, 1.0 / 6.0], [1.0 / 6.0, 1.0 / 3.0]])
    mass = np.kron(np.kron(line, line), line)
    return stiff, mass


def factors():
    stiff, mass = hex_matrices()
    pair = np.array([[1.0, 1.0], [-1.0, 1.0]])
    modes = np.kron(np.kron(pair, pair), pair)
    mass_weight = np.sqrt(np.diag(modes @ mass @ modes.T) / 64.0)
    both = np.kron(modes, np.eye(3))
    blocks = both @ stiff @ both.T / 64.0
    rows = []
    for label in range(8):
        index = [(label ^ (4 >> comp)) * 3 + comp for comp in range(3)]
        block = blocks[np.ix_(index, index)].copy()
        for k in range(3):
            if block[k, k] > 1e-9:
                row = block[k] / math.sqrt(block[k, k])
                rows.append([(index[b], float(row[b])) for b in range(3) if abs(row[b]) > 1e-9])
                block -= np.outer(row, row)
        assert np.abs(block).max() < 1e-9
    return mass_weight, rows


def pack_body(group, comps, planes, plane, chunks, x_ref, out_ref):
    stride = x_ref.shape[0] // group
    width_y = stride // (comps * planes)
    own = width_y // chunks
    for comp in range(comps):
        for y in range(width_y):
            start = (comp * planes + plane) * width_y + y
            value = x_ref[pl.ds(start, group, stride=stride), :]
            out_ref[y // own, comp * (own + 1) + y % own] = value
            if y % own == 0:
                out_ref[(y // own - 1) % chunks, comp * (own + 1) + own] = value


def pack_plane(basis, plane, chunks):
    group, comps, planes, width_y, width_z = basis.shape
    own = width_y // chunks
    return pl.pallas_call(
        functools.partial(pack_body, group, comps, planes, plane, chunks),
        out_shape=jax.ShapeDtypeStruct((chunks, comps * (own + 1), group, width_z), F32),
        in_specs=[pl.BlockSpec(memory_space=VMEM)],
        out_specs=pl.BlockSpec(memory_space=VMEM),
        name="pack",
    )(basis.reshape(-1, width_z))


def gram_body(scale, r0_ref, r1_ref, r2_ref, w_ref, out_ref, z_ref, mass_ref, stiff_ref):
    mass_weight, stiff_rows = factors()
    planes = (r0_ref, r1_ref, r2_ref)
    columns = 192
    n_mass = 24 * 128
    mass_ref[...] = jnp.zeros_like(mass_ref)
    stiff_ref[...] = jnp.zeros_like(stiff_ref)
    for i in range(2):
        for j in range(2):
            root = w_ref[0, i, pl.ds(j, 1), :]
            cubed = w_ref[1, i, pl.ds(j, 1), :]

            def step(q, carry):
                for g in range(3):
                    modes = {}
                    for comp in range(3):
                        lines = {}
                        for a in range(2):
                            for b in range(2):
                                parts = []
                                for n in (2 * g, 2 * g + 1):
                                    t = n % 3
                                    parts.append(
                                        planes[i + a][2 * q + n // 3, comp * 3 + j + b, 8 * t : 8 * t + 8, :]
                                    )
                                here = jnp.concatenate(parts, axis=0)
                                there = pltpu.roll(here, 127, 1)
                                lines[a, b, 0] = here + there
                                lines[a, b, 1] = there - here
                        faces = {}
                        for a in range(2):
                            for pc in range(2):
                                faces[a, 0, pc] = lines[a, 1, pc] + lines[a, 0, pc]
                                faces[a, 1, pc] = lines[a, 1, pc] - lines[a, 0, pc]
                        for pb in range(2):
                            for pc in range(2):
                                low, high = faces[0, pb, pc], faces[1, pb, pc]
                                modes[(2 * pb + pc) * 3 + comp] = high + low
                                modes[(4 + 2 * pb + pc) * 3 + comp] = high - low
                    start = pl.multiple_of(q * 48 + g * 16, 16)

                    def put(slot, value):
                        high = value.astype(BF16)
                        low = (value - high.astype(F32)).astype(BF16)
                        z_ref[pl.ds(start, 16), slot * 128 : slot * 128 + 128] = high
                        z_ref[pl.ds(columns + start, 16), slot * 128 : slot * 128 + 128] = low

                    for mode in range(24):
                        put(mode, modes[mode] * (root * float(mass_weight[mode // 3])))
                    for number, row in enumerate(stiff_rows):
                        total = None
                        for mode, coef in row:
                            term = modes[mode] * (cubed * coef)
                            total = term if total is None else total + term
                        put(24 + number, total)
                return carry

            lax.fori_loop(0, 4, step, 0)
            contract = (((1,), (1,)), ((), ()))
            mass_ref[...] += lax.dot_general(
                z_ref[:, :n_mass], z_ref[:columns, :n_mass], contract, preferred_element_type=F32
            )
            stiff_ref[...] += lax.dot_general(
                z_ref[:, n_mass:], z_ref[:columns, n_mass:], contract, preferred_element_type=F32
            )

    def whole(ref):
        cross = ref[columns:, :]
        return (ref[:columns, :] + cross + cross.T) * scale

    mass, stiff = whole(mass_ref), whole(stiff_ref)
    row = lax.broadcasted_iota(jnp.int32, (columns, columns), 0)
    col = lax.broadcasted_iota(jnp.int32, (columns, columns), 1)
    mixed = jnp.where(row >= col, stiff, mass)
    diagonal = jnp.sum(jnp.where(row == col, mass, 0.0), axis=1, keepdims=True)
    out_ref[:columns, :] = mixed[:, :128]
    out_ref[columns:, :64] = mixed[:, 128:]
    out_ref[columns:, 64:] = jnp.broadcast_to(diagonal, (columns, 64))


def gram(r0, r1, r2, weights, scale):
    slots = 24 + len(factors()[1])
    return pl.pallas_call(
        functools.partial(gram_body, scale),
        out_shape=jax.ShapeDtypeStruct((384, 128), F32),
        in_specs=[pl.BlockSpec(memory_space=VMEM)] * 4,
        out_specs=pl.BlockSpec(memory_space=VMEM),
        scratch_shapes=[
            VMEM((384, slots * 128), BF16),
            VMEM((384, 192), F32),
            VMEM((384, 192), F32),
        ],
        compiler_params=pltpu.CompilerParams(vmem_limit_bytes=48 * 2**20),
        name="gram",
    )(r0, r1, r2, weights)


def dot32(a, b, contract=((1,), (0,))):
    return lax.dot_general(
        a, b, (contract, ((), ())), precision=lax.Precision.HIGHEST, preferred_element_type=F32
    )


def eliminate(block):
    size = block.shape[0]
    row = lax.broadcasted_iota(jnp.int32, (size, size), 0)
    col = lax.broadcasted_iota(jnp.int32, (size, size), 1)
    unit = jnp.where(row == col, 1.0, 0.0).astype(F32)
    work = jnp.concatenate([block, unit], axis=1)
    pieces = [work[8 * t : 8 * t + 8, :] for t in range(size // 8)]
    sub = lax.broadcasted_iota(jnp.int32, (8, 128), 0)
    for j in range(size):
        at, inner = j // 8, j % 8
        line = pieces[at][inner : inner + 1, :]
        ratio = line / line[:, j : j + 1]
        for t in range(at, size // 8):
            factor = pieces[t][:, j : j + 1]
            change = factor * ratio
            if t == at:
                change = jnp.where(sub > inner, change, 0.0)
            pieces[t] = pieces[t] - change
    work = jnp.concatenate(pieces, axis=0)
    pivots = jnp.sum(jnp.where(row == col, work[:, :size], 0.0), axis=1, keepdims=True)
    root = lax.rsqrt(pivots)
    root = root * (1.5 - 0.5 * pivots * root * root)
    return work[:, size:] * root


def split(value):
    high = value.astype(BF16)
    return high, (value - high.astype(F32)).astype(BF16)


def solve_body(g_ref, r0_ref, r1_ref, send_ref, inverse_ref, stiff_ref, a_ref):
    columns, size = 192, 64
    packed = g_ref[...].reshape(384, 128)
    mixed = jnp.concatenate([packed[:columns], packed[columns:, :64]], axis=1)
    diagonal = packed[columns:, 64:65]
    row = lax.broadcasted_iota(jnp.int32, (columns, columns), 0)
    col = lax.broadcasted_iota(jnp.int32, (columns, columns), 1)
    other = mixed.T
    stiff_ref[...] = jnp.where(row >= col, mixed, other)
    mass = jnp.where(row < col, mixed, jnp.where(row == col, diagonal, other))
    a_ref[...] = jnp.zeros_like(a_ref)
    a_ref[:, :columns] = mass
    a_ref[:, 256 : 256 + columns] = jnp.where(row == col, 1.0, 0.0).astype(F32)
    for k in range(columns // size):
        low, high = k * size, k * size + size
        lines = dot32(eliminate(a_ref[low:high, low:high]), a_ref[low:high, :])
        a_ref[low:high, :] = lines
        if high < columns:
            a_ref[high:, :] -= dot32(lines[:, high:columns], lines, ((0,), (0,)))
    inverse = a_ref[:, 256 : 256 + columns]
    inverse_ref[...] = inverse
    left_high, left_low = split(inverse)
    for plane, ref in enumerate((r0_ref, r1_ref)):
        for comp in range(3):
            pair = [ref[:, comp * 3 + j].reshape(columns, 128) for j in range(2)]
            right_high, right_low = split(jnp.concatenate(pair, axis=1))
            total = jnp.dot(left_high, right_high, preferred_element_type=F32)
            total += jnp.dot(left_high, right_low, preferred_element_type=F32)
            total += jnp.dot(left_low, right_high, preferred_element_type=F32)
            for j in range(2):
                slot = (comp * 2 + plane) * 2 + j
                send_ref[:, slot] = total[:, 128 * j : 128 * j + 128].reshape(8, 24, 128)


def solve(packed, r0, r1):
    return pl.pallas_call(
        solve_body,
        out_shape=(
            jax.ShapeDtypeStruct((8, 12, 24, 128), F32),
            jax.ShapeDtypeStruct((192, 192), F32),
            jax.ShapeDtypeStruct((192, 192), F32),
        ),
        in_specs=[pl.BlockSpec(memory_space=VMEM)] * 3,
        out_specs=[pl.BlockSpec(memory_space=VMEM)] * 3,
        scratch_shapes=[VMEM((192, 512), F32)],
        compiler_params=pltpu.CompilerParams(vmem_limit_bytes=48 * 2**20),
        name="solve",
    )(packed, r0, r1)


def unpack_body(t_ref, out_ref):
    for source in range(8):
        for comp in range(3):
            for plane in range(2):
                for j in range(2):
                    start = (comp * 2 + plane) * 16 + 2 * source + j
                    slot = (comp * 2 + plane) * 2 + j
                    out_ref[pl.ds(start, 24, stride=96), :] = t_ref[source, slot]


def unpack(received):
    return pl.pallas_call(
        unpack_body,
        out_shape=jax.ShapeDtypeStruct((2304, 128), F32),
        in_specs=[pl.BlockSpec(memory_space=VMEM)],
        out_specs=pl.BlockSpec(memory_space=VMEM),
        name="unpack",
    )(received)


def exchange(value, axes):
    return lax.all_to_all(value, axes, 0, 0)


def copies(value, count):
    return jnp.broadcast_to(value[None], (count,) + value.shape)


def per_device(basis, density):
    chunks = lax.axis_size(MODE)
    slabs = lax.axis_size(SPACE)
    width_y = basis.shape[3]
    own = width_y // chunks
    scale = 1.0 / (3.0 * basis.shape[2] * width_y * basis.shape[4] * slabs)
    density = lax.dynamic_slice_in_dim(density, lax.axis_index(MODE) * own, own, axis=1)
    root = jnp.sqrt(density)
    weights = jnp.stack([root, density * root])

    r0 = exchange(pack_plane(basis, 0, chunks), MODE)
    second, r0 = lax.optimization_barrier((pack_plane(basis, 1, chunks), r0))
    r2 = lax.ppermute(r0, SPACE, [(i, i - 1) for i in range(1, slabs)])
    r1 = exchange(second, MODE)
    part = gram(r0, r1, r2, weights, scale)

    plane_axes, line_axes = MODE + ("yh",), ("zc",)
    first, last = lax.axis_size(plane_axes), lax.axis_size(line_axes)
    piece = exchange(part.reshape(first, 384 // first, 128), plane_axes).sum(0)
    piece = exchange(copies(piece, last), line_axes).sum(0)
    packed = exchange(copies(piece, first), plane_axes)

    send, inverse, stiff = solve(packed, r0, r1)
    rotated = unpack(exchange(send, MODE)).reshape(basis.shape)
    high = lax.Precision.HIGHEST
    reduced = jnp.dot(jnp.dot(inverse, stiff, precision=high), inverse.T, precision=high)
    return rotated, reduced


def solution(mesh):
    modes, slabs = mesh.devices.shape
    half = 2 if slabs % 4 == 0 else 1
    inner = Mesh(mesh.devices.reshape(modes // 2, 2, half, slabs // half), MODE + SPACE)
    field = P(MODE, None, SPACE, None, None)
    return jax.shard_map(
        per_device,
        mesh=inner,
        in_specs=(field, P(SPACE, None, None)),
        out_specs=(field, P()),
        check_vma=False,
    )
```

profile of v0, /device:TPU:8, one launch (start us, length us, event | category | flops | bytes accessed | tf_op | source)
XLA Modules:
  0.0 145.8 jit_solution(7864086849208140388)
XLA Ops:
  0.6 2.5 %pack.3 = f32[8,9,24,128]{3,2,1,0:T(8,128)} custom-call(f32[2304,128]{1,0:T(8,128)} %bitcast.12), custom_call_target="tpu_custom_call" | custom-call | tf_op jit(solution)/shard_map/pack/pallas_call | solution.py:93
  3.2 5.8 %all-to-all-start = ((f32[8,9,24,128]{3,2,1,0:T(8,128)}), f32[8,9,24,128]{3,2,1,0:T(8,128)S(1)}, u32[]{:S(2)}, u32[]{:S(2)}) async-start(f32[8,9,24,128]{3,2,1,0:T(8,128)} %pack.3), calls=%async_computation | async-start | bytes 1769472 | tf_op jit(solution)/shard_map/all_to_all | solution.py:306
  8.9 2.5 %pack.2 = f32[8,9,24,128]{3,2,1,0:T(8,128)} custom-call(f32[2304,128]{1,0:T(8,128)} %bitcast.13), custom_call_target="tpu_custom_call" | custom-call | tf_op jit(solution)/shard_map/pack/pallas_call | solution.py:93
  11.4 10.3 %all-to-all-done.r0_ref = f32[8,9,24,128]{3,2,1,0:T(8,128)S(1)} async-done(((f32[8,9,24,128]{3,2,1,0:T(8,128)}), f32[8,9,24,128]{3,2,1,0:T(8,128)S(1)}, u32[]{:S(2)}, u32[]{:S(2)}) %all-to-all-start) | async-done | bytes 884768 | tf_op jit(solution)/shard_map/all_to_all | solution.py:306
  21.7 1.3 collective-permute-start
  23.0 4.2 %all-to-all-start.1 = ((f32[8,9,24,128]{3,2,1,0:T(8,128)}), f32[8,9,24,128]{3,2,1,0:T(8,128)S(1)}, u32[]{:S(2)}, u32[]{:S(2)}) async-start(f32[8,9,24,128]{3,2,1,0:T(8,128)} %pack.2), calls=%async_computation.1 | async-start | bytes 1769472 | tf_op jit(solution)/shard_map/all_to_all | solution.py:306
  27.3 0.7 sqrt_bitcast_fusion
  28.0 15.1 %all-to-all-done.1.r1_ref = f32[8,9,24,128]{3,2,1,0:T(8,128)S(1)} async-done(((f32[8,9,24,128]{3,2,1,0:T(8,128)}), f32[8,9,24,128]{3,2,1,0:T(8,128)S(1)}, u32[]{:S(2)}, u32[]{:S(2)}) %all-to-all-start.1) | async-done | bytes 884768 | tf_op jit(solution)/shard_map/all_to_all | solution.py:306
  43.1 0.0 collective-permute-done.r2_ref
  43.1 11.8 %gram.1 = f32[384,128]{1,0:T(8,128)S(1)} custom-call(f32[8,9,24,128]{3,2,1,0:T(8,128)S(1)} %all-to-all-done.r0_ref, f32[8,9,24,128]{3,2,1,0:T(8,128)S(1)} %all-to-all-done.1.r1_ref, f32[8,9,24,128]{3,2,1,0:T(8,128)S(1)} %collective-permute-done.r2_ref, f32[2,2,2,128]{3,2,1,0:T(2,128)S(1)} %pad_maximum_fusion.w_ref), custom_call_target="tpu_custom_call" | custom-call | tf_op jit(solution)/shard_map/gram/pallas_call | solution.py:184
  54.9 13.5 %all_to_all.30 = f32[16,24,128]{2,1,0:T(8,128)S(1)} all-to-all(f32[16,24,128]{2,1,0:T(8,128)S(1)} %bitcast.11), channel_id=1, replica_groups=mesh['x'=4,'yl'=2,'yh'=2,'zc'=16] {'x','yl','yh'}, dimensions={0} | all-to-all | bytes 393216 | tf_op jit(solution)/shard_map/all_to_all | solution.py:306
  68.5 20.6 %all_to_all.31 = f32[16,24,128]{2,1,0:T(8,128)S(1)} all-to-all(f32[16,24,128]{2,1,0:T(8,128)S(1)} %broadcast_in_dim.4), channel_id=1, replica_groups=mesh['x'=4,'yl'=2,'yh'=2,'zc'=16] {'zc'}, dimensions={0} | all-to-all | bytes 393216 | tf_op jit(solution)/shard_map/all_to_all | solution.py:306
  89.1 12.2 %all_to_all.32.g_ref = f32[16,24,128]{2,1,0:T(8,128)S(1)} all-to-all(f32[16,24,128]{2,1,0:T(8,128)S(1)} %broadcast_in_dim.5), channel_id=1, replica_groups=mesh['x'=4,'yl'=2,'yh'=2,'zc'=16] {'x','yl','yh'}, dimensions={0} | all-to-all | bytes 393216 | tf_op jit(solution)/shard_map/all_to_all | solution.py:306
  101.3 19.5 %solve.1 = (f32[8,12,24,128]{3,2,1,0:T(8,128)}, f32[192,192]{1,0:T(8,128)S(1)}, f32[192,192]{1,0:T(8,128)S(1)}) custom-call(f32[16,24,128]{2,1,0:T(8,128)S(1)} %all_to_all.32.g_ref, f32[8,9,24,128]{3,2,1,0:T(8,128)S(1)} %all-to-all-done.r0_ref, f32[8,9,24,128]{3,2,1,0:T(8,128)S(1)} %all-to-all-done.1.r1_ref), custom_call_target="tpu_custom_call" | custom-call | tf_op jit(solution)/shard_map/solve/pallas_call | solution.py:270
  120.8 4.9 %all-to-all-start.5 = ((f32[8,12,24,128]{3,2,1,0:T(8,128)}), f32[8,12,24,128]{3,2,1,0:T(8,128)S(1)}, u32[]{:S(2)}, u32[]{:S(2)}) async-start(f32[8,12,24,128]{3,2,1,0:T(8,128)} %get-tuple-element.9), calls=%async_computation.5 | async-start | bytes 2359296 | tf_op jit(solution)/shard_map/all_to_all | solution.py:306
  125.7 0.3 fusion.1
  126.0 1.0 fusion.2
  127.0 14.4 %all-to-all-done.5.t_ref = f32[8,12,24,128]{3,2,1,0:T(8,128)S(1)} async-done(((f32[8,12,24,128]{3,2,1,0:T(8,128)}), f32[8,12,24,128]{3,2,1,0:T(8,128)S(1)}, u32[]{:S(2)}, u32[]{:S(2)}) %all-to-all-start.5) | async-done | bytes 1179680 | tf_op jit(solution)/shard_map/all_to_all | solution.py:306
  141.4 0.0 copy-start
  141.4 1.0 copy-done
  142.5 3.3 %unpack.1 = f32[2304,128]{1,0:T(8,128)} custom-call(f32[8,12,24,128]{3,2,1,0:T(8,128)} %copy-done), custom_call_target="tpu_custom_call" | custom-call | tf_op jit(solution)/shard_map/unpack/pallas_call | solution.py:296
  (5 shorter events, 0.1 us)
Async XLA Ops:
  3.2 18.6 %all-to-all-start = ((f32[8,9,24,128]{3,2,1,0:T(8,128)}), f32[8,9,24,128]{3,2,1,0:T(8,128)S(1)}, u32[]{:S(2)}, u32[]{:S(2)}) async-start(f32[8,9,24,128]{3,2,1,0:T(8,128)} %pack.3), calls=%async_computation | async-start | bytes 1769472 | tf_op jit(solution)/shard_map/all_to_all | solution.py:306
  21.7 21.3 %collective-permute-start = (f32[8,9,24,128]{3,2,1,0:T(8,128)S(1)}, f32[8,9,24,128]{3,2,1,0:T(8,128)S(1)}, u32[]{:S(2)}, u32[]{:S(2)}) collective-permute-start(f32[8,9,24,128]{3,2,1,0:T(8,128)S(1)} %all-to-all-done.r0_ref), channel_id=1, source_target_pairs={{1,0},{2,1},{3,2},{4,3},{5,4},{6,5},{7,6},{8,7},{9,8},{10,9},{11,1... | collective-permute-start | bytes 2654216 | tf_op jit(solution)/shard_map/ppermute | solution.py:325
  23.0 20.0 %all-to-all-start.1 = ((f32[8,9,24,128]{3,2,1,0:T(8,128)}), f32[8,9,24,128]{3,2,1,0:T(8,128)S(1)}, u32[]{:S(2)}, u32[]{:S(2)}) async-start(f32[8,9,24,128]{3,2,1,0:T(8,128)} %pack.2), calls=%async_computation.1 | async-start | bytes 1769472 | tf_op jit(solution)/shard_map/all_to_all | solution.py:306
  120.8 20.7 %all-to-all-start.5 = ((f32[8,12,24,128]{3,2,1,0:T(8,128)}), f32[8,12,24,128]{3,2,1,0:T(8,128)S(1)}, u32[]{:S(2)}, u32[]{:S(2)}) async-start(f32[8,12,24,128]{3,2,1,0:T(8,128)} %get-tuple-element.9), calls=%async_computation.5 | async-start | bytes 2359296 | tf_op jit(solution)/shard_map/all_to_all | solution.py:306
  141.4 1.0 copy-start
where the time goes:
time: 147 us; the launch traced here: 146 us
  blocking collectives  46.3 us (31%)
  waiting for transfers between devices  39.8 us (27%)
  Pallas kernels  39.7 us (27%)
  starting transfers between devices  16.2 us (11%)
    all_to_all x3, blocking collectives, exchange(): return lax.all_to_all(value, axes, 0, 0)  46.3 us
    all_to_all x3, waiting for transfers between devices, exchange(): return lax.all_to_all(value, axes, 0, 0)  39.8 us
    pallas_call x1, Pallas kernels, solve(): pl.pallas_call(solve_body, out_shape=(jax.ShapeDtypeStruct((8, 12, 24, 12...  19.5 us
    all_to_all x3, starting transfers between devices, exchange(): return lax.all_to_all(value, axes, 0, 0)  14.9 us
    pallas_call x1, Pallas kernels, gram(): pl.pallas_call(functools.partial(gram_body, scale), out_shape=jax.ShapeDt...  11.8 us
    pallas_call x2, Pallas kernels, pack_plane(): pl.pallas_call(functools.partial(pack_body, group, comps, planes, plane,...  5.06 us
    pallas_call x1, Pallas kernels, unpack(): pl.pallas_call(unpack_body, out_shape=jax.ShapeDtypeStruct((2304, 128), F...  3.34 us
  transfers between devices with their start and end apart: 4, of which 3 were waited for; matrix products, arithmetic and copies ran while one was open for 1% of the time, Pallas kernels for 2%

commit v1 on v0

--- a/solution.py
+++ b/solution.py
@@ -204,27 +204,33 @@
 
 def eliminate(block):
     size = block.shape[0]
-    row = lax.broadcasted_iota(jnp.int32, (size, size), 0)
-    col = lax.broadcasted_iota(jnp.int32, (size, size), 1)
-    unit = jnp.where(row == col, 1.0, 0.0).astype(F32)
-    work = jnp.concatenate([block, unit], axis=1)
-    pieces = [work[8 * t : 8 * t + 8, :] for t in range(size // 8)]
+    groups = size // 8
     sub = lax.broadcasted_iota(jnp.int32, (8, 128), 0)
-    for j in range(size):
-        at, inner = j // 8, j % 8
-        line = pieces[at][inner : inner + 1, :]
-        ratio = line / line[:, j : j + 1]
-        for t in range(at, size // 8):
-            factor = pieces[t][:, j : j + 1]
-            change = factor * ratio
-            if t == at:
-                change = jnp.where(sub > inner, change, 0.0)
-            pieces[t] = pieces[t] - change
-    work = jnp.concatenate(pieces, axis=0)
-    pivots = jnp.sum(jnp.where(row == col, work[:, :size], 0.0), axis=1, keepdims=True)
-    root = lax.rsqrt(pivots)
-    root = root * (1.5 - 0.5 * pivots * root * root)
-    return work[:, size:] * root
+    lane = lax.broadcasted_iota(jnp.int32, (8, 128), 1)
+    spread = {}
+    for k in range(size):
+        for t in range(k // 8, groups):
+            spread[k, t] = jnp.broadcast_to(block[8 * t : 8 * t + 8, k : k + 1], (8, 128))
+    right = [jnp.where(lane == sub + 8 * t, 1.0, 0.0).astype(F32) for t in range(groups)]
+    for i in range(size):
+        at, inner = i // 8, i % 8
+        inverse = 1.0 / spread[i, at][inner : inner + 1, :]
+        factor = {t: spread[i, t] * inverse for t in range(at, groups)}
+        factor[at] = jnp.where(sub > inner, factor[at], 0.0)
+        for k in range(i + 1, size):
+            entry = spread[i, k // 8][k % 8 : k % 8 + 1, :]
+            for t in range(k // 8, groups):
+                spread[k, t] = spread[k, t] - factor[t] * entry
+        line = right[at][inner : inner + 1, :]
+        for t in range(at, groups):
+            right[t] = right[t] - factor[t] * line
+    for t in range(groups):
+        pivots = spread[8 * t, t]
+        for inner in range(1, 8):
+            pivots = jnp.where(sub == inner, spread[8 * t + inner, t], pivots)
+        root = lax.rsqrt(pivots)
+        right[t] = right[t] * (root * (1.5 - 0.5 * pivots * root * root))
+    return jnp.concatenate(right, axis=0)[:, :size]
 
 
 def split(value):
@@ -233,7 +239,7 @@
 
 
 def solve_body(g_ref, r0_ref, r1_ref, send_ref, inverse_ref, stiff_ref, a_ref):
-    columns, size = 192, 64
+    columns, size = 192, 32
     packed = g_ref[...].reshape(384, 128)
     mixed = jnp.concatenate([packed[:columns], packed[columns:, :64]], axis=1)
     diagonal = packed[columns:, 64:65]

time: 147 us -> 137 us (0.932)
  Pallas kernels: 39.7 us -> 29 us
    pallas_call x1, Pallas kernels: 19.5 us -> 8.73 us  [solve(): pl.pallas_call(solve_body, out_shape=(jax.ShapeDtypeStruct((8, 12, 24, 12...]
  transfers between devices with their start and end apart: 4 -> 4, of which waited for: 3 -> 3; matrix products, arithmetic and copies ran while one was open for 1% -> 2% of each run, Pallas kernels for 2% -> 2%
where the time goes in v1:
time: 137 us; the launch traced here: 135 us
  blocking collectives  46.3 us (34%)
  waiting for transfers between devices  39.8 us (29%)
  Pallas kernels  29 us (21%)
  starting transfers between devices  16.2 us (12%)
    all_to_all x3, blocking collectives, exchange(): return lax.all_to_all(value, axes, 0, 0)  46.3 us
    all_to_all x3, waiting for transfers between devices, exchange(): return lax.all_to_all(value, axes, 0, 0)  39.8 us
    all_to_all x3, starting transfers between devices, exchange(): return lax.all_to_all(value, axes, 0, 0)  14.9 us
    pallas_call x1, Pallas kernels, gram(): pl.pallas_call(functools.partial(gram_body, scale), out_shape=jax.ShapeDt...  11.8 us
    pallas_call x1, Pallas kernels, solve(): pl.pallas_call(solve_body, out_shape=(jax.ShapeDtypeStruct((8, 12, 24, 12...  8.73 us
    pallas_call x2, Pallas kernels, pack_plane(): pl.pallas_call(functools.partial(pack_body, group, comps, planes, plane,...  5.06 us
    pallas_call x1, Pallas kernels, unpack(): pl.pallas_call(unpack_body, out_shape=jax.ShapeDtypeStruct((2304, 128), F...  3.34 us
  transfers between devices with their start and end apart: 4, of which 3 were waited for; matrix products, arithmetic and copies ran while one was open for 2% of the time, Pallas kernels for 2%

profile of v1, /device:TPU:8, one launch (start us, length us, event | category | flops | bytes accessed | tf_op | source)
XLA Modules:
  0.0 135.1 jit_solution(8750431303552576526)
XLA Ops:
  0.6 2.5 %pack.3 = f32[8,9,24,128]{3,2,1,0:T(8,128)} custom-call(f32[2304,128]{1,0:T(8,128)} %bitcast.12), custom_call_target="tpu_custom_call" | custom-call | tf_op jit(solution)/shard_map/pack/pallas_call | solution.py:93
  3.2 5.8 %all-to-all-start = ((f32[8,9,24,128]{3,2,1,0:T(8,128)}), f32[8,9,24,128]{3,2,1,0:T(8,128)S(1)}, u32[]{:S(2)}, u32[]{:S(2)}) async-start(f32[8,9,24,128]{3,2,1,0:T(8,128)} %pack.3), calls=%async_computation | async-start | bytes 1769472 | tf_op jit(solution)/shard_map/all_to_all | solution.py:312
  8.9 2.5 %pack.2 = f32[8,9,24,128]{3,2,1,0:T(8,128)} custom-call(f32[2304,128]{1,0:T(8,128)} %bitcast.13), custom_call_target="tpu_custom_call" | custom-call | tf_op jit(solution)/shard_map/pack/pallas_call | solution.py:93
  11.4 10.3 %all-to-all-done.r0_ref = f32[8,9,24,128]{3,2,1,0:T(8,128)S(1)} async-done(((f32[8,9,24,128]{3,2,1,0:T(8,128)}), f32[8,9,24,128]{3,2,1,0:T(8,128)S(1)}, u32[]{:S(2)}, u32[]{:S(2)}) %all-to-all-start) | async-done | bytes 884768 | tf_op jit(solution)/shard_map/all_to_all | solution.py:312
  21.7 1.3 collective-permute-start
  23.0 4.2 %all-to-all-start.1 = ((f32[8,9,24,128]{3,2,1,0:T(8,128)}), f32[8,9,24,128]{3,2,1,0:T(8,128)S(1)}, u32[]{:S(2)}, u32[]{:S(2)}) async-start(f32[8,9,24,128]{3,2,1,0:T(8,128)} %pack.2), calls=%async_computation.1 | async-start | bytes 1769472 | tf_op jit(solution)/shard_map/all_to_all | solution.py:312
  27.3 0.7 sqrt_bitcast_fusion
  28.0 15.1 %all-to-all-done.1.r1_ref = f32[8,9,24,128]{3,2,1,0:T(8,128)S(1)} async-done(((f32[8,9,24,128]{3,2,1,0:T(8,128)}), f32[8,9,24,128]{3,2,1,0:T(8,128)S(1)}, u32[]{:S(2)}, u32[]{:S(2)}) %all-to-all-start.1) | async-done | bytes 884768 | tf_op jit(solution)/shard_map/all_to_all | solution.py:312
  43.1 0.0 collective-permute-done.r2_ref
  43.1 11.8 %gram.1 = f32[384,128]{1,0:T(8,128)S(1)} custom-call(f32[8,9,24,128]{3,2,1,0:T(8,128)S(1)} %all-to-all-done.r0_ref, f32[8,9,24,128]{3,2,1,0:T(8,128)S(1)} %all-to-all-done.1.r1_ref, f32[8,9,24,128]{3,2,1,0:T(8,128)S(1)} %collective-permute-done.r2_ref, f32[2,2,2,128]{3,2,1,0:T(2,128)S(1)} %pad_maximum_fusion.w_ref), custom_call_target="tpu_custom_call" | custom-call | tf_op jit(solution)/shard_map/gram/pallas_call | solution.py:184
  54.9 13.5 %all_to_all.30 = f32[16,24,128]{2,1,0:T(8,128)S(1)} all-to-all(f32[16,24,128]{2,1,0:T(8,128)S(1)} %bitcast.11), channel_id=1, replica_groups=mesh['x'=4,'yl'=2,'yh'=2,'zc'=16] {'x','yl','yh'}, dimensions={0} | all-to-all | bytes 393216 | tf_op jit(solution)/shard_map/all_to_all | solution.py:312
  68.5 20.6 %all_to_all.31 = f32[16,24,128]{2,1,0:T(8,128)S(1)} all-to-all(f32[16,24,128]{2,1,0:T(8,128)S(1)} %broadcast_in_dim.4), channel_id=1, replica_groups=mesh['x'=4,'yl'=2,'yh'=2,'zc'=16] {'zc'}, dimensions={0} | all-to-all | bytes 393216 | tf_op jit(solution)/shard_map/all_to_all | solution.py:312
  89.1 12.2 %all_to_all.32.g_ref = f32[16,24,128]{2,1,0:T(8,128)S(1)} all-to-all(f32[16,24,128]{2,1,0:T(8,128)S(1)} %broadcast_in_dim.5), channel_id=1, replica_groups=mesh['x'=4,'yl'=2,'yh'=2,'zc'=16] {'x','yl','yh'}, dimensions={0} | all-to-all | bytes 393216 | tf_op jit(solution)/shard_map/all_to_all | solution.py:312
  101.3 8.7 %solve.1 = (f32[8,12,24,128]{3,2,1,0:T(8,128)}, f32[192,192]{1,0:T(8,128)S(1)}, f32[192,192]{1,0:T(8,128)S(1)}) custom-call(f32[16,24,128]{2,1,0:T(8,128)S(1)} %all_to_all.32.g_ref, f32[8,9,24,128]{3,2,1,0:T(8,128)S(1)} %all-to-all-done.r0_ref, f32[8,9,24,128]{3,2,1,0:T(8,128)S(1)} %all-to-all-done.1.r1_ref), custom_call_target="tpu_custom_call" | custom-call | tf_op jit(solution)/shard_map/solve/pallas_call | solution.py:276
  110.0 4.9 %all-to-all-start.5 = ((f32[8,12,24,128]{3,2,1,0:T(8,128)}), f32[8,12,24,128]{3,2,1,0:T(8,128)S(1)}, u32[]{:S(2)}, u32[]{:S(2)}) async-start(f32[8,12,24,128]{3,2,1,0:T(8,128)} %get-tuple-element.9), calls=%async_computation.5 | async-start | bytes 2359296 | tf_op jit(solution)/shard_map/all_to_all | solution.py:312
  114.9 0.3 fusion.1
  115.3 1.0 fusion.2
  116.3 14.4 %all-to-all-done.5.t_ref = f32[8,12,24,128]{3,2,1,0:T(8,128)S(1)} async-done(((f32[8,12,24,128]{3,2,1,0:T(8,128)}), f32[8,12,24,128]{3,2,1,0:T(8,128)S(1)}, u32[]{:S(2)}, u32[]{:S(2)}) %all-to-all-start.5) | async-done | bytes 1179680 | tf_op jit(solution)/shard_map/all_to_all | solution.py:312
  130.7 0.0 copy-start
  130.7 1.0 copy-done
  131.7 3.3 %unpack.1 = f32[2304,128]{1,0:T(8,128)} custom-call(f32[8,12,24,128]{3,2,1,0:T(8,128)} %copy-done), custom_call_target="tpu_custom_call" | custom-call | tf_op jit(solution)/shard_map/unpack/pallas_call | solution.py:302
  (5 shorter events, 0.1 us)
Async XLA Ops:
  3.2 18.6 %all-to-all-start = ((f32[8,9,24,128]{3,2,1,0:T(8,128)}), f32[8,9,24,128]{3,2,1,0:T(8,128)S(1)}, u32[]{:S(2)}, u32[]{:S(2)}) async-start(f32[8,9,24,128]{3,2,1,0:T(8,128)} %pack.3), calls=%async_computation | async-start | bytes 1769472 | tf_op jit(solution)/shard_map/all_to_all | solution.py:312
  21.7 21.3 %collective-permute-start = (f32[8,9,24,128]{3,2,1,0:T(8,128)S(1)}, f32[8,9,24,128]{3,2,1,0:T(8,128)S(1)}, u32[]{:S(2)}, u32[]{:S(2)}) collective-permute-start(f32[8,9,24,128]{3,2,1,0:T(8,128)S(1)} %all-to-all-done.r0_ref), channel_id=1, source_target_pairs={{1,0},{2,1},{3,2},{4,3},{5,4},{6,5},{7,6},{8,7},{9,8},{10,9},{11,1... | collective-permute-start | bytes 2654216 | tf_op jit(solution)/shard_map/ppermute | solution.py:331
  23.0 20.0 %all-to-all-start.1 = ((f32[8,9,24,128]{3,2,1,0:T(8,128)}), f32[8,9,24,128]{3,2,1,0:T(8,128)S(1)}, u32[]{:S(2)}, u32[]{:S(2)}) async-start(f32[8,9,24,128]{3,2,1,0:T(8,128)} %pack.2), calls=%async_computation.1 | async-start | bytes 1769472 | tf_op jit(solution)/shard_map/all_to_all | solution.py:312
  110.0 20.7 %all-to-all-start.5 = ((f32[8,12,24,128]{3,2,1,0:T(8,128)}), f32[8,12,24,128]{3,2,1,0:T(8,128)S(1)}, u32[]{:S(2)}, u32[]{:S(2)}) async-start(f32[8,12,24,128]{3,2,1,0:T(8,128)} %get-tuple-element.9), calls=%async_computation.5 | async-start | bytes 2359296 | tf_op jit(solution)/shard_map/all_to_all | solution.py:312
  130.7 1.0 copy-start

commit v2 on v1

v2 whole, which is shorter than its diff:
```python
import functools
import math

import jax
import jax.numpy as jnp
import numpy as np
from jax import lax
from jax.experimental import pallas as pl
from jax.experimental.pallas import tpu as pltpu
from jax.sharding import Mesh, PartitionSpec as P

VMEM = pltpu.VMEM
MODE = ("x", "yl")
SPACE = ("yh", "zc")
F32 = jnp.float32
BF16 = jnp.bfloat16


def hex_matrices():
    poisson = 0.3
    lame_first = poisson / ((1.0 + poisson) * (1.0 - 2.0 * poisson))
    shear = 1.0 / (2.0 * (1.0 + poisson))
    elastic = np.zeros((6, 6))
    elastic[:3, :3] = lame_first
    for number in range(3):
        elastic[number, number] += 2.0 * shear
        elastic[number + 3, number + 3] = shear
    points = [0.5 - 0.5 / math.sqrt(3.0), 0.5 + 0.5 / math.sqrt(3.0)]
    corners = [(a, b, c) for a in (0, 1) for b in (0, 1) for c in (0, 1)]
    stiff = np.zeros((24, 24))
    for point_x in points:
        for point_y in points:
            for point_z in points:
                strain = np.zeros((6, 24))
                for number, corner in enumerate(corners):
                    shape_x = point_x if corner[0] else 1.0 - point_x
                    shape_y = point_y if corner[1] else 1.0 - point_y
                    shape_z = point_z if corner[2] else 1.0 - point_z
                    deriv_x = (2.0 * corner[0] - 1.0) * shape_y * shape_z
                    deriv_y = shape_x * (2.0 * corner[1] - 1.0) * shape_z
                    deriv_z = shape_x * shape_y * (2.0 * corner[2] - 1.0)
                    strain[0, 3 * number] = deriv_x
                    strain[1, 3 * number + 1] = deriv_y
                    strain[2, 3 * number + 2] = deriv_z
                    strain[3, 3 * number] = deriv_y
                    strain[3, 3 * number + 1] = deriv_x
                    strain[4, 3 * number + 1] = deriv_z
                    strain[4, 3 * number + 2] = deriv_y
                    strain[5, 3 * number] = deriv_z
                    strain[5, 3 * number + 2] = deriv_x
                stiff += strain.T @ elastic @ strain / 8.0
    line = np.array([[1.0 / 3.0, 1.0 / 6.0], [1.0 / 6.0, 1.0 / 3.0]])
    mass = np.kron(np.kron(line, line), line)
    return stiff, mass


def factors():
    stiff, mass = hex_matrices()
    pair = np.array([[1.0, 1.0], [-1.0, 1.0]])
    modes = np.kron(np.kron(pair, pair), pair)
    mass_weight = np.sqrt(np.diag(modes @ mass @ modes.T) / 64.0)
    both = np.kron(modes, np.eye(3))
    blocks = both @ stiff @ both.T / 64.0
    rows = []
    for label in range(8):
        index = [(label ^ (4 >> comp)) * 3 + comp for comp in range(3)]
        block = blocks[np.ix_(index, index)].copy()
        for k in range(3):
            if block[k, k] > 1e-9:
                row = block[k] / math.sqrt(block[k, k])
                rows.append([(index[b], float(row[b])) for b in range(3) if abs(row[b]) > 1e-9])
                block -= np.outer(row, row)
        assert np.abs(block).max() < 1e-9
    return mass_weight, rows


def swap_blocks(vectors):
    block = lax.broadcasted_iota(jnp.int32, vectors[0].shape, 1) // 16
    vectors = [pltpu.roll(v, 16 * k, 1) if k else v for k, v in enumerate(vectors)]
    for step in (1, 2, 4):
        moved = (block & step) != 0
        vectors = [jnp.where(moved, vectors[(k + step) % 8], vectors[k]) for k in range(8)]
    return [pltpu.roll(vectors[-k % 8], 128 - 16 * k, 1) if k else vectors[0] for k in range(8)]


def slot_of(plane, comp, half):
    return (1 - plane) * 6 + comp * 2 + half


def edge_lane(plane, comp, half):
    return half * 6 + plane * 3 + comp


def pack_body(x_ref, out_ref):
    for plane in range(2):
        for comp in range(3):
            first = (comp * 2 + plane) * 16
            lines = jnp.swapaxes(x_ref[:, first : first + 16, :], 0, 1)
            for half in range(2):
                parts = swap_blocks([lines[2 * k + half] for k in range(8)])
                for chunk in range(8):
                    out_ref[chunk, slot_of(plane, comp, half)] = parts[chunk]
    within = lax.broadcasted_iota(jnp.int32, (24, 128), 1) % 16
    for chunk in range(8):
        edge = jnp.zeros((24, 128), F32)
        for plane in range(2):
            for comp in range(3):
                for half in range(2):
                    lane = edge_lane(plane, comp, half)
                    value = out_ref[(chunk + 1) % 8, slot_of(plane, comp, half)]
                    edge = jnp.where(within == lane, pltpu.roll(value, lane, 1), edge)
        out_ref[chunk, 12] = edge


def pack(basis):
    return pl.pallas_call(
        pack_body,
        out_shape=jax.ShapeDtypeStruct((8, 13, 24, 128), F32),
        in_specs=[pl.BlockSpec(memory_space=VMEM)],
        out_specs=pl.BlockSpec(memory_space=VMEM),
        name="pack",
    )(basis.reshape(24, 96, 128))


def gram_body(scale, layer, near_ref, far_ref, w_ref, *rest):
    if layer == 0:
        before_ref, (out_ref, mass_ref, stiff_ref) = None, rest
        places = ((near_ref, 0, 0), (near_ref, 1, 0))
    else:
        before_ref, out_ref, mass_ref, stiff_ref = rest
        places = ((near_ref, 1, 0), (far_ref, 0, 6))
    mass_weight, stiff_rows = factors()
    columns = 192
    last = lax.broadcasted_iota(jnp.int32, (16, 128), 1) % 16 == 15

    def read(ref, q, g, slot):
        parts = []
        for n in (2 * g, 2 * g + 1):
            t = n % 3
            parts.append(ref[2 * q + n // 3, slot, 8 * t : 8 * t + 8, :])
        return jnp.concatenate(parts, axis=0)

    def step(q, carry):
        for g in range(3):
            modes = {}
            edges = [read(ref, q, g, 12 - back) for ref, _, back in places]
            for comp in range(3):
                faces = {}
                for a, (ref, plane, back) in enumerate(places):
                    lines = {}
                    for half in range(2):
                        here = read(ref, q, g, slot_of(plane, comp, half) - back)
                        edge = pltpu.roll(edges[a], 15 - edge_lane(plane, comp, half), 1)
                        there = jnp.where(last, edge, pltpu.roll(here, 127, 1))
                        lines[half, 0] = here + there
                        lines[half, 1] = there - here
                    for pc in range(2):
                        even, odd = lines[0, pc], lines[1, pc]
                        following = pltpu.roll(even, 112, 1)
                        faces[a, 0, 0, pc] = odd + even
                        faces[a, 0, 1, pc] = odd - even
                        faces[a, 1, 0, pc] = following + odd
                        faces[a, 1, 1, pc] = following - odd
                for half in range(2):
                    for pb in range(2):
                        for pc in range(2):
                            low, high = faces[0, half, pb, pc], faces[1, half, pb, pc]
                            modes[half, (2 * pb + pc) * 3 + comp] = high + low
                            modes[half, (4 + 2 * pb + pc) * 3 + comp] = high - low
            start = pl.multiple_of(q * 48 + g * 16, 16)

            def put(ref, slot, value):
                high = value.astype(BF16)
                low = (value - high.astype(F32)).astype(BF16)
                ref[pl.ds(start, 16), slot * 128 : slot * 128 + 128] = high
                ref[pl.ds(columns + start, 16), slot * 128 : slot * 128 + 128] = low

            for half in range(2):
                root = w_ref[0, layer, pl.ds(half, 1), :]
                cubed = w_ref[1, layer, pl.ds(half, 1), :]
                for mode in range(24):
                    value = modes[half, mode] * (root * float(mass_weight[mode // 3]))
                    put(mass_ref, 24 * half + mode, value)
                for number, row in enumerate(stiff_rows):
                    total = None
                    for mode, coef in row:
                        term = modes[half, mode] * (cubed * coef)
                        total = term if total is None else total + term
                    put(stiff_ref, len(stiff_rows) * half + number, total)
        return carry

    lax.fori_loop(0, 4, step, 0)

    def whole(ref):
        both = lax.dot_general(
            ref[...], ref[:columns, :], (((1,), (1,)), ((), ())), preferred_element_type=F32
        )
        cross = both[columns:, :]
        return (both[:columns, :] + cross + cross.T) * scale

    mass, stiff = whole(mass_ref), whole(stiff_ref)
    row = lax.broadcasted_iota(jnp.int32, (columns, columns), 0)
    col = lax.broadcasted_iota(jnp.int32, (columns, columns), 1)
    mixed = jnp.where(row >= col, stiff, mass)
    diagonal = jnp.sum(jnp.where(row == col, mass, 0.0), axis=1, keepdims=True)
    out_ref[:columns, :] = mixed[:, :128]
    out_ref[columns:, :64] = mixed[:, 128:]
    out_ref[columns:, 64:] = jnp.broadcast_to(diagonal, (columns, 64))
    if before_ref is not None:
        out_ref[...] += before_ref[...]


def gram(layer, near, far, weights, scale, before=()):
    stiff = len(factors()[1])
    return pl.pallas_call(
        functools.partial(gram_body, scale, layer),
        out_shape=jax.ShapeDtypeStruct((384, 128), F32),
        in_specs=[pl.BlockSpec(memory_space=VMEM)] * (3 + len(before)),
        out_specs=pl.BlockSpec(memory_space=VMEM),
        scratch_shapes=[
            VMEM((384, 2 * 24 * 128), BF16),
            VMEM((384, 2 * stiff * 128), BF16),
        ],
        compiler_params=pltpu.CompilerParams(vmem_limit_bytes=48 * 2**20),
        cost_estimate=pl.CostEstimate(flops=3 * 10**9, bytes_accessed=3 * 10**6, transcendentals=0),
        name="gram",
    )(near, far, weights, *before)


def dot32(a, b, contract=((1,), (0,))):
    return lax.dot_general(
        a, b, (contract, ((), ())), precision=lax.Precision.HIGHEST, preferred_element_type=F32
    )


def eliminate(block):
    size = block.shape[0]
    groups = size // 8
    sub = lax.broadcasted_iota(jnp.int32, (8, 128), 0)
    lane = lax.broadcasted_iota(jnp.int32, (8, 128), 1)
    spread = {}
    for k in range(size):
        for t in range(k // 8, groups):
            spread[k, t] = jnp.broadcast_to(block[8 * t : 8 * t + 8, k : k + 1], (8, 128))
    right = [jnp.where(lane == sub + 8 * t, 1.0, 0.0).astype(F32) for t in range(groups)]
    for i in range(size):
        at, inner = i // 8, i % 8
        inverse = 1.0 / spread[i, at][inner : inner + 1, :]
        factor = {t: spread[i, t] * inverse for t in range(at, groups)}
        factor[at] = jnp.where(sub > inner, factor[at], 0.0)
        for k in range(i + 1, size):
            entry = spread[i, k // 8][k % 8 : k % 8 + 1, :]
            for t in range(k // 8, groups):
                spread[k, t] = spread[k, t] - factor[t] * entry
        line = right[at][inner : inner + 1, :]
        for t in range(at, groups):
            right[t] = right[t] - factor[t] * line
    for t in range(groups):
        pivots = spread[8 * t, t]
        for inner in range(1, 8):
            pivots = jnp.where(sub == inner, spread[8 * t + inner, t], pivots)
        root = lax.rsqrt(pivots)
        right[t] = right[t] * (root * (1.5 - 0.5 * pivots * root * root))
    return jnp.concatenate(right, axis=0)[:, :size]


def split(value):
    high = value.astype(BF16)
    return high, (value - high.astype(F32)).astype(BF16)


def solve_body(g_ref, r_ref, send_ref, inverse_ref, stiff_ref, a_ref):
    columns, size = 192, 32
    packed = g_ref[...].reshape(384, 128)
    mixed = jnp.concatenate([packed[:columns], packed[columns:, :64]], axis=1)
    diagonal = packed[columns:, 64:65]
    row = lax.broadcasted_iota(jnp.int32, (columns, columns), 0)
    col = lax.broadcasted_iota(jnp.int32, (columns, columns), 1)
    other = mixed.T
    stiff_ref[...] = jnp.where(row >= col, mixed, other)
    mass = jnp.where(row < col, mixed, jnp.where(row == col, diagonal, other))
    a_ref[...] = jnp.zeros_like(a_ref)
    a_ref[:, :columns] = mass
    a_ref[:, 256 : 256 + columns] = jnp.where(row == col, 1.0, 0.0).astype(F32)
    for k in range(columns // size):
        low, high = k * size, k * size + size
        lines = dot32(eliminate(a_ref[low:high, low:high]), a_ref[low:high, :])
        a_ref[low:high, :] = lines
        if high < columns:
            a_ref[high:, :] -= dot32(lines[:, high:columns], lines, ((0,), (0,)))
    inverse = a_ref[:, 256 : 256 + columns]
    inverse_ref[...] = inverse
    left_high, left_low = split(inverse)
    for pair in range(6):
        sides = [r_ref[:, 2 * pair + half].reshape(columns, 128) for half in range(2)]
        right_high, right_low = split(jnp.concatenate(sides, axis=1))
        total = jnp.dot(left_high, right_high, preferred_element_type=F32)
        total += jnp.dot(left_high, right_low, preferred_element_type=F32)
        total += jnp.dot(left_low, right_high, preferred_element_type=F32)
        for half in range(2):
            send_ref[:, 2 * pair + half] = total[:, 128 * half : 128 * half + 128].reshape(8, 24, 128)


def solve(packed, received):
    return pl.pallas_call(
        solve_body,
        out_shape=(
            jax.ShapeDtypeStruct((8, 12, 24, 128), F32),
            jax.ShapeDtypeStruct((192, 192), F32),
            jax.ShapeDtypeStruct((192, 192), F32),
        ),
        in_specs=[pl.BlockSpec(memory_space=VMEM)] * 2,
        out_specs=[pl.BlockSpec(memory_space=VMEM)] * 3,
        scratch_shapes=[VMEM((192, 512), F32)],
        compiler_params=pltpu.CompilerParams(vmem_limit_bytes=48 * 2**20),
        name="solve",
    )(packed, received)


def unpack_body(t_ref, out_ref):
    for plane in range(2):
        for comp in range(3):
            lines = [None] * 16
            for half in range(2):
                slot = slot_of(plane, comp, half)
                lines[half::2] = swap_blocks([t_ref[chunk, slot] for chunk in range(8)])
            first = (comp * 2 + plane) * 16
            out_ref[:, first : first + 16, :] = jnp.swapaxes(jnp.stack(lines), 0, 1)


def unpack(received):
    return pl.pallas_call(
        unpack_body,
        out_shape=jax.ShapeDtypeStruct((24, 96, 128), F32),
        in_specs=[pl.BlockSpec(memory_space=VMEM)],
        out_specs=pl.BlockSpec(memory_space=VMEM),
        name="unpack",
    )(received)


def exchange(value, axes):
    return lax.all_to_all(value, axes, 0, 0)


def copies(value, count):
    return jnp.broadcast_to(value[None], (count,) + value.shape)


def per_device(basis, density):
    chunks = lax.axis_size(MODE)
    slabs = lax.axis_size(SPACE)
    planes, width_y, width_z = basis.shape[2:]
    own = width_z // chunks
    scale = 1.0 / (3.0 * planes * width_y * width_z * slabs)
    density = lax.dynamic_slice_in_dim(density, lax.axis_index(MODE) * own, own, axis=2)
    density = jnp.swapaxes(density.reshape(planes, width_y // 2, 2, own), 1, 2)
    density = density.reshape(planes, 2, width_y // 2 * own)
    root = jnp.sqrt(density)
    weights = jnp.stack([root, density * root])

    near = exchange(pack(basis), MODE)
    far = lax.ppermute(near[:, 6:], SPACE, [(i, i - 1) for i in range(1, slabs)])
    part = gram(0, near, near, weights, scale)
    part = gram(1, near, far, weights, scale, (part,))

    plane_axes, line_axes = MODE + ("yh",), ("zc",)
    first, last = lax.axis_size(plane_axes), lax.axis_size(line_axes)
    piece = exchange(part.reshape(first, 384 // first, 128), plane_axes).sum(0)
    piece = exchange(copies(piece, last), line_axes).sum(0)
    packed = exchange(copies(piece, first), plane_axes)

    send, inverse, stiff = solve(packed, near)
    rotated = unpack(exchange(send, MODE)).reshape(basis.shape)
    high = lax.Precision.HIGHEST
    reduced = jnp.dot(jnp.dot(inverse, stiff, precision=high), inverse.T, precision=high)
    return rotated, reduced


def solution(mesh):
    modes, slabs = mesh.devices.shape
    half = 2 if slabs % 4 == 0 else 1
    inner = Mesh(mesh.devices.reshape(modes // 2, 2, half, slabs // half), MODE + SPACE)
    field = P(MODE, None, SPACE, None, None)
    return jax.shard_map(
        per_device,
        mesh=inner,
        in_specs=(field, P(SPACE, None, None)),
        out_specs=(field, P()),
        check_vma=False,
    )
```

time: 137 us -> 124 us (0.905)
  waiting for transfers between devices: 39.8 us -> 31.7 us
  starting transfers between devices: 16.2 us -> 12 us
  Pallas kernels: 29 us -> 27 us
  blocking collectives: 46.3 us -> 48.2 us
    all_to_all x3 -> x2, waiting for transfers between devices: 39.8 us -> 31.7 us  [exchange(): return lax.all_to_all(value, axes, 0, 0)]
    all_to_all x3 -> x2, starting transfers between devices: 14.9 us -> 10.7 us  [exchange(): return lax.all_to_all(value, axes, 0, 0)]
    pallas_call x4, Pallas kernels: 20.2 us -> 18.2 us  [the longest x2 10.8 us: gram(): pl.pallas_call(functools.partial(gram_body, scale, layer), out_shape=jax....]
    all_to_all x3, blocking collectives: 46.3 us -> 48.2 us  [exchange(): return lax.all_to_all(value, axes, 0, 0)]
  transfers between devices with their start and end apart: 4 -> 3, of which waited for: 3 -> 2; matrix products, arithmetic and copies ran while one was open for 2% -> 1% of each run, Pallas kernels for 2% -> 4%
where the time goes in v2:
time: 124 us; the launch traced here: 122 us
  blocking collectives  48.2 us (39%)
  waiting for transfers between devices  31.7 us (26%)
  Pallas kernels  27 us (22%)
  starting transfers between devices  12 us (10%)
  matrix products  1.34 us (1%)
  local copies, waits for them, and re-layouts  1.27 us (1%)
    all_to_all x3, blocking collectives, exchange(): return lax.all_to_all(value, axes, 0, 0)  48.2 us
    all_to_all x2, waiting for transfers between devices, exchange(): return lax.all_to_all(value, axes, 0, 0)  31.7 us
    pallas_call x2, Pallas kernels, gram(): pl.pallas_call(functools.partial(gram_body, scale, layer), out_shape=jax....  10.8 us
    all_to_all x2, starting transfers between devices, exchange(): return lax.all_to_all(value, axes, 0, 0)  10.7 us
    pallas_call x1, Pallas kernels, solve(): pl.pallas_call(solve_body, out_shape=(jax.ShapeDtypeStruct((8, 12, 24, 12...  8.73 us
    pallas_call x1, Pallas kernels, pack(): pl.pallas_call(pack_body, out_shape=jax.ShapeDtypeStruct((8, 13, 24, 128)...  3.94 us
    pallas_call x1, Pallas kernels, unpack(): pl.pallas_call(unpack_body, out_shape=jax.ShapeDtypeStruct((24, 96, 128),...  3.55 us
  transfers between devices with their start and end apart: 3, of which 2 were waited for; matrix products, arithmetic and copies ran while one was open for 1% of the time, Pallas kernels for 4%

profile of v2, /device:TPU:8, one launch (start us, length us, event | category | flops | bytes accessed | tf_op | source)
XLA Modules:
  0.0 122.3 jit_solution(10643185032413746029)
XLA Ops:
  0.6 0.0 copy-start
  0.6 3.9 %pack.1 = f32[8,13,24,128]{3,2,1,0:T(8,128)} custom-call(f32[24,96,128]{2,1,0:T(8,128)} %bitcast.13), custom_call_target="tpu_custom_call" | custom-call | tf_op jit(solution)/shard_map/pack/pallas_call | solution.py:116
  4.6 5.8 %all-to-all-start = ((f32[8,13,24,128]{3,2,1,0:T(8,128)}), f32[8,13,24,128]{3,2,1,0:T(8,128)S(1)}, u32[]{:S(2)}, u32[]{:S(2)}) async-start(f32[8,13,24,128]{3,2,1,0:T(8,128)} %pack.1), calls=%async_computation | async-start | bytes 2555904 | tf_op jit(solution)/shard_map/all_to_all | solution.py:342
  10.3 17.3 %all-to-all-done.near_ref.far_ref.r_ref = f32[8,13,24,128]{3,2,1,0:T(8,128)S(1)} async-done(((f32[8,13,24,128]{3,2,1,0:T(8,128)}), f32[8,13,24,128]{3,2,1,0:T(8,128)S(1)}, u32[]{:S(2)}, u32[]{:S(2)}) %all-to-all-start) | async-done | bytes 1277984 | tf_op jit(solution)/shard_map/all_to_all | solution.py:342
  27.7 1.3 %collective-permute-start = (f32[8,7,24,128]{3,2,1,0:T(8,128)S(1)}, f32[8,7,24,128]{3,2,1,0:T(8,128)S(1)}, u32[]{:S(2)}, u32[]{:S(2)}) collective-permute-start(f32[8,7,24,128]{3,2,1,0:T(8,128)S(1)} %slice.4), channel_id=1, source_target_pairs={{1,0},{2,1},{3,2},{4,3},{5,4},{6,5},{7,6},{8,7},{9,8},{10,9},{11,1... | collective-permute-start | bytes 2064392 | tf_op jit(solution)/shard_map/ppermute | solution.py:362
  29.0 0.0 copy-done
  29.0 0.1 constant_dynamic-slice_fusion
  29.1 0.1 reshape.46
  29.2 5.4 %gram.2.rest_0_ = f32[384,128]{1,0:T(8,128)S(1)} custom-call(f32[8,13,24,128]{3,2,1,0:T(8,128)S(1)} %all-to-all-done.near_ref.far_ref.r_ref, f32[8,13,24,128]{3,2,1,0:T(8,128)S(1)} %all-to-all-done.near_ref.far_ref.r_ref, f32[2,2,2,128]{3,2,1,0:T(2,128)S(1)} %pad_maximum_fusion.w_ref), custom_call_target="tpu_custom_call" | custom-call | flops 3000000000 | bytes 3000000 | tf_op jit(solution)/shard_map/gram/pallas_call | solution.py:215
  34.6 0.0 collective-permute-done.far_ref
  34.6 5.4 %gram.3 = f32[384,128]{1,0:T(8,128)S(1)} custom-call(f32[8,13,24,128]{3,2,1,0:T(8,128)S(1)} %all-to-all-done.near_ref.far_ref.r_ref, f32[8,7,24,128]{3,2,1,0:T(8,128)S(1)} %collective-permute-done.far_ref, f32[2,2,2,128]{3,2,1,0:T(2,128)S(1)} %pad_maximum_fusion.w_ref, f32[384,128]{1,0:T(8,128)S(1)} %gram.2.rest_0_), custom_call_target="tpu_custom_call" | custom-call | flops 3000000000 | bytes 3000000 | tf_op jit(solution)/shard_map/gram/pallas_call | solution.py:215
  40.0 21.6 %all_to_all.25 = f32[16,24,128]{2,1,0:T(8,128)S(1)} all-to-all(f32[16,24,128]{2,1,0:T(8,128)S(1)} %bitcast.12), channel_id=1, replica_groups=mesh['x'=4,'yl'=2,'yh'=2,'zc'=16] {'x','yl','yh'}, dimensions={0} | all-to-all | bytes 393216 | tf_op jit(solution)/shard_map/all_to_all | solution.py:342
  61.6 14.3 %all_to_all.26 = f32[16,24,128]{2,1,0:T(8,128)S(1)} all-to-all(f32[16,24,128]{2,1,0:T(8,128)S(1)} %broadcast_in_dim.4), channel_id=1, replica_groups=mesh['x'=4,'yl'=2,'yh'=2,'zc'=16] {'zc'}, dimensions={0} | all-to-all | bytes 393216 | tf_op jit(solution)/shard_map/all_to_all | solution.py:342
  76.0 12.3 %all_to_all.27.g_ref = f32[16,24,128]{2,1,0:T(8,128)S(1)} all-to-all(f32[16,24,128]{2,1,0:T(8,128)S(1)} %broadcast_in_dim.5), channel_id=1, replica_groups=mesh['x'=4,'yl'=2,'yh'=2,'zc'=16] {'x','yl','yh'}, dimensions={0} | all-to-all | bytes 393216 | tf_op jit(solution)/shard_map/all_to_all | solution.py:342
  88.3 8.7 %solve.1 = (f32[8,12,24,128]{3,2,1,0:T(8,128)}, f32[192,192]{1,0:T(8,128)S(1)}, f32[192,192]{1,0:T(8,128)S(1)}) custom-call(f32[16,24,128]{2,1,0:T(8,128)S(1)} %all_to_all.27.g_ref, f32[8,13,24,128]{3,2,1,0:T(8,128)S(1)} %all-to-all-done.near_ref.far_ref.r_ref), custom_call_target="tpu_custom_call" | custom-call | tf_op jit(solution)/shard_map/solve/pallas_call | solution.py:305
  97.0 4.9 %all-to-all-start.4 = ((f32[8,12,24,128]{3,2,1,0:T(8,128)}), f32[8,12,24,128]{3,2,1,0:T(8,128)S(1)}, u32[]{:S(2)}, u32[]{:S(2)}) async-start(f32[8,12,24,128]{3,2,1,0:T(8,128)} %get-tuple-element.5), calls=%async_computation.4 | async-start | bytes 2359296 | tf_op jit(solution)/shard_map/all_to_all | solution.py:342
  101.9 0.3 fusion.1
  102.3 1.0 fusion.2
  103.3 14.4 %all-to-all-done.4.t_ref = f32[8,12,24,128]{3,2,1,0:T(8,128)S(1)} async-done(((f32[8,12,24,128]{3,2,1,0:T(8,128)}), f32[8,12,24,128]{3,2,1,0:T(8,128)S(1)}, u32[]{:S(2)}, u32[]{:S(2)}) %all-to-all-start.4) | async-done | bytes 1179680 | tf_op jit(solution)/shard_map/all_to_all | solution.py:342
  117.7 0.0 copy-start.1
  117.7 1.0 copy-done.1
  118.7 3.6 %unpack.1 = f32[24,96,128]{2,1,0:T(8,128)} custom-call(f32[8,12,24,128]{3,2,1,0:T(8,128)} %copy-done.1), custom_call_target="tpu_custom_call" | custom-call | tf_op jit(solution)/shard_map/unpack/pallas_call | solution.py:332
  (8 shorter events, 0.1 us)
Async XLA Ops:
  0.6 28.4 %copy-start = (f32[2,16,128]{2,1,0:T(8,128)S(1)}, f32[2,16,128]{2,1,0:T(8,128)}, u32[]{:S(2)}) copy-start(f32[2,16,128]{2,1,0:T(8,128)} %param.3) | copy-start | bytes 49156
  4.6 23.1 %all-to-all-start = ((f32[8,13,24,128]{3,2,1,0:T(8,128)}), f32[8,13,24,128]{3,2,1,0:T(8,128)S(1)}, u32[]{:S(2)}, u32[]{:S(2)}) async-start(f32[8,13,24,128]{3,2,1,0:T(8,128)} %pack.1), calls=%async_computation | async-start | bytes 2555904 | tf_op jit(solution)/shard_map/all_to_all | solution.py:342
  27.7 6.9 %collective-permute-start = (f32[8,7,24,128]{3,2,1,0:T(8,128)S(1)}, f32[8,7,24,128]{3,2,1,0:T(8,128)S(1)}, u32[]{:S(2)}, u32[]{:S(2)}) collective-permute-start(f32[8,7,24,128]{3,2,1,0:T(8,128)S(1)} %slice.4), channel_id=1, source_target_pairs={{1,0},{2,1},{3,2},{4,3},{5,4},{6,5},{7,6},{8,7},{9,8},{10,9},{11,1... | collective-permute-start | bytes 2064392 | tf_op jit(solution)/shard_map/ppermute | solution.py:362
  97.0 20.7 %all-to-all-start.4 = ((f32[8,12,24,128]{3,2,1,0:T(8,128)}), f32[8,12,24,128]{3,2,1,0:T(8,128)S(1)}, u32[]{:S(2)}, u32[]{:S(2)}) async-start(f32[8,12,24,128]{3,2,1,0:T(8,128)} %get-tuple-element.5), calls=%async_computation.4 | async-start | bytes 2359296 | tf_op jit(solution)/shard_map/all_to_all | solution.py:342
  117.7 1.0 copy-start.1

commit v3 on v2

--- a/solution.py
+++ b/solution.py
@@ -11,7 +11,7 @@
 
 VMEM = pltpu.VMEM
 MODE = ("x", "yl")
-SPACE = ("yh", "zc")
+SPACE = ("yh", "z", "core")
 F32 = jnp.float32
 BF16 = jnp.bfloat16
 
@@ -83,15 +83,21 @@
     return [pltpu.roll(vectors[-k % 8], 128 - 16 * k, 1) if k else vectors[0] for k in range(8)]
 
 
-def slot_of(plane, comp, half):
-    return (1 - plane) * 6 + comp * 2 + half
+def slot_of(comp, half):
+    return comp * 2 + half
 
 
 def edge_lane(plane, comp, half):
     return half * 6 + plane * 3 + comp
 
 
-def pack_body(x_ref, out_ref):
+def turned(chunk, turn):
+    return chunk + turn if chunk % 2 == 0 else chunk - turn
+
+
+def pack_body(turn_ref, x_ref, out0_ref, out1_ref):
+    outs = (out0_ref, out1_ref)
+    turn = turn_ref[0]
     for plane in range(2):
         for comp in range(3):
             first = (comp * 2 + plane) * 16
@@ -99,7 +105,7 @@
             for half in range(2):
                 parts = swap_blocks([lines[2 * k + half] for k in range(8)])
                 for chunk in range(8):
-                    out_ref[chunk, slot_of(plane, comp, half)] = parts[chunk]
+                    outs[plane][turned(chunk, turn), slot_of(comp, half)] = parts[chunk]
     within = lax.broadcasted_iota(jnp.int32, (24, 128), 1) % 16
     for chunk in range(8):
         edge = jnp.zeros((24, 128), F32)
@@ -107,28 +113,32 @@
             for comp in range(3):
                 for half in range(2):
                     lane = edge_lane(plane, comp, half)
-                    value = out_ref[(chunk + 1) % 8, slot_of(plane, comp, half)]
+                    value = outs[plane][turned((chunk + 1) % 8, turn), slot_of(comp, half)]
                     edge = jnp.where(within == lane, pltpu.roll(value, lane, 1), edge)
-        out_ref[chunk, 12] = edge
-
-
-def pack(basis):
+        out0_ref[turned(chunk, turn), 6] = edge
+
+
+def pack(turn, basis):
     return pl.pallas_call(
         pack_body,
-        out_shape=jax.ShapeDtypeStruct((8, 13, 24, 128), F32),
-        in_specs=[pl.BlockSpec(memory_space=VMEM)],
-        out_specs=pl.BlockSpec(memory_space=VMEM),
+        out_shape=(
+            jax.ShapeDtypeStruct((8, 7, 24, 128), F32),
+            jax.ShapeDtypeStruct((8, 6, 24, 128), F32),
+        ),
+        in_specs=[pl.BlockSpec(memory_space=pltpu.SMEM), pl.BlockSpec(memory_space=VMEM)],
+        out_specs=[pl.BlockSpec(memory_space=VMEM)] * 2,
+        compiler_params=pltpu.CompilerParams(vmem_limit_bytes=12 * 2**20),
         name="pack",
-    )(basis.reshape(24, 96, 128))
-
-
-def gram_body(scale, layer, near_ref, far_ref, w_ref, *rest):
+    )(turn, basis.reshape(24, 96, 128))
+
+
+def gram_body(scale, layer, first_ref, second_ref, edge_ref, w_ref, *rest):
     if layer == 0:
         before_ref, (out_ref, mass_ref, stiff_ref) = None, rest
-        places = ((near_ref, 0, 0), (near_ref, 1, 0))
+        places = ((first_ref, first_ref, 0), (second_ref, first_ref, 1))
     else:
         before_ref, out_ref, mass_ref, stiff_ref = rest
-        places = ((near_ref, 1, 0), (far_ref, 0, 6))
+        places = ((first_ref, edge_ref, 1), (second_ref, second_ref, 0))
     mass_weight, stiff_rows = factors()
     columns = 192
     last = lax.broadcasted_iota(jnp.int32, (16, 128), 1) % 16 == 15
@@ -143,13 +153,13 @@
     def step(q, carry):
         for g in range(3):
             modes = {}
-            edges = [read(ref, q, g, 12 - back) for ref, _, back in places]
+            edges = [read(edge, q, g, 6) for _, edge, _ in places]
             for comp in range(3):
                 faces = {}
-                for a, (ref, plane, back) in enumerate(places):
+                for a, (ref, _, plane) in enumerate(places):
                     lines = {}
                     for half in range(2):
-                        here = read(ref, q, g, slot_of(plane, comp, half) - back)
+                        here = read(ref, q, g, slot_of(comp, half))
                         edge = pltpu.roll(edges[a], 15 - edge_lane(plane, comp, half), 1)
                         there = jnp.where(last, edge, pltpu.roll(here, 127, 1))
                         lines[half, 0] = here + there
@@ -210,21 +220,21 @@
         out_ref[...] += before_ref[...]
 
 
-def gram(layer, near, far, weights, scale, before=()):
+def gram(layer, first, second, edge, weights, scale, before=()):
     stiff = len(factors()[1])
     return pl.pallas_call(
         functools.partial(gram_body, scale, layer),
         out_shape=jax.ShapeDtypeStruct((384, 128), F32),
-        in_specs=[pl.BlockSpec(memory_space=VMEM)] * (3 + len(before)),
+        in_specs=[pl.BlockSpec(memory_space=VMEM)] * (4 + len(before)),
         out_specs=pl.BlockSpec(memory_space=VMEM),
         scratch_shapes=[
             VMEM((384, 2 * 24 * 128), BF16),
             VMEM((384, 2 * stiff * 128), BF16),
         ],
-        compiler_params=pltpu.CompilerParams(vmem_limit_bytes=48 * 2**20),
+        compiler_params=pltpu.CompilerParams(vmem_limit_bytes=20 * 2**20),
         cost_estimate=pl.CostEstimate(flops=3 * 10**9, bytes_accessed=3 * 10**6, transcendentals=0),
         name="gram",
-    )(near, far, weights, *before)
+    )(first, second, edge, weights, *before)
 
 
 def dot32(a, b, contract=((1,), (0,))):
@@ -233,15 +243,14 @@
     )
 
 
-def eliminate(block):
-    size = block.shape[0]
+def eliminate(block, first, size):
     groups = size // 8
     sub = lax.broadcasted_iota(jnp.int32, (8, 128), 0)
     lane = lax.broadcasted_iota(jnp.int32, (8, 128), 1)
     spread = {}
     for k in range(size):
         for t in range(k // 8, groups):
-            spread[k, t] = jnp.broadcast_to(block[8 * t : 8 * t + 8, k : k + 1], (8, 128))
+            spread[k, t] = jnp.broadcast_to(block[8 * t : 8 * t + 8, first + k : first + k + 1], (8, 128))
     right = [jnp.where(lane == sub + 8 * t, 1.0, 0.0).astype(F32) for t in range(groups)]
     for i in range(size):
         at, inner = i // 8, i % 8
@@ -269,7 +278,7 @@
     return high, (value - high.astype(F32)).astype(BF16)
 
 
-def solve_body(g_ref, r_ref, send_ref, inverse_ref, stiff_ref, a_ref):
+def solve_body(g_ref, r0_ref, r1_ref, send_ref, inverse_ref, stiff_ref):
     columns, size = 192, 32
     packed = g_ref[...].reshape(384, 128)
     mixed = jnp.concatenate([packed[:columns], packed[columns:, :64]], axis=1)
@@ -279,29 +288,43 @@
     other = mixed.T
     stiff_ref[...] = jnp.where(row >= col, mixed, other)
     mass = jnp.where(row < col, mixed, jnp.where(row == col, diagonal, other))
-    a_ref[...] = jnp.zeros_like(a_ref)
-    a_ref[:, :columns] = mass
-    a_ref[:, 256 : 256 + columns] = jnp.where(row == col, 1.0, 0.0).astype(F32)
-    for k in range(columns // size):
-        low, high = k * size, k * size + size
-        lines = dot32(eliminate(a_ref[low:high, low:high]), a_ref[low:high, :])
-        a_ref[low:high, :] = lines
-        if high < columns:
-            a_ref[high:, :] -= dot32(lines[:, high:columns], lines, ((0,), (0,)))
-    inverse = a_ref[:, 256 : 256 + columns]
+    unit = jnp.where(row == col, 1.0, 0.0).astype(F32)
+    count = columns // size
+    left = [mass[k * size : k * size + size] for k in range(count)]
+    right = [unit[k * size : k * size + size] for k in range(count)]
+    done = []
+    for k in range(count):
+        root = eliminate(left[k], k * size, size)
+        line = dot32(root, left[k])
+        if k + 1 < count:
+            turned_line = line.T
+            left[k + 1] = left[k + 1] - dot32(turned_line[(k + 1) * size : (k + 2) * size], line)
+        ready = dot32(root, right[k])
+        done.append(ready)
+        if k + 1 < count:
+            both = dot32(turned_line[(k + 1) * size :], ready)
+            for i in range(k + 1, count):
+                right[i] = right[i] - both[(i - k - 1) * size : (i - k) * size]
+        if k + 2 < count:
+            both = dot32(turned_line[(k + 2) * size :], line)
+            for i in range(k + 2, count):
+                left[i] = left[i] - both[(i - k - 2) * size : (i - k - 1) * size]
+    inverse = jnp.concatenate(done, axis=0)
     inverse_ref[...] = inverse
     left_high, left_low = split(inverse)
-    for pair in range(6):
-        sides = [r_ref[:, 2 * pair + half].reshape(columns, 128) for half in range(2)]
-        right_high, right_low = split(jnp.concatenate(sides, axis=1))
-        total = jnp.dot(left_high, right_high, preferred_element_type=F32)
-        total += jnp.dot(left_high, right_low, preferred_element_type=F32)
-        total += jnp.dot(left_low, right_high, preferred_element_type=F32)
-        for half in range(2):
-            send_ref[:, 2 * pair + half] = total[:, 128 * half : 128 * half + 128].reshape(8, 24, 128)
-
-
-def solve(packed, received):
+    for plane, ref in enumerate((r0_ref, r1_ref)):
+        for comp in range(3):
+            sides = [ref[:, slot_of(comp, half)].reshape(columns, 128) for half in range(2)]
+            right_high, right_low = split(jnp.concatenate(sides, axis=1))
+            total = jnp.dot(left_high, right_high, preferred_element_type=F32)
+            total += jnp.dot(left_high, right_low, preferred_element_type=F32)
+            total += jnp.dot(left_low, right_high, preferred_element_type=F32)
+            for half in range(2):
+                part = total[:, 128 * half : 128 * half + 128].reshape(8, 24, 128)
+                send_ref[:, plane * 6 + slot_of(comp, half)] = part
+
+
+def solve(packed, first, second):
     return pl.pallas_call(
         solve_body,
         out_shape=(
@@ -309,33 +332,43 @@
             jax.ShapeDtypeStruct((192, 192), F32),
             jax.ShapeDtypeStruct((192, 192), F32),
         ),
-        in_specs=[pl.BlockSpec(memory_space=VMEM)] * 2,
+        in_specs=[pl.BlockSpec(memory_space=VMEM)] * 3,
         out_specs=[pl.BlockSpec(memory_space=VMEM)] * 3,
-        scratch_shapes=[VMEM((192, 512), F32)],
-        compiler_params=pltpu.CompilerParams(vmem_limit_bytes=48 * 2**20),
+        compiler_params=pltpu.CompilerParams(vmem_limit_bytes=20 * 2**20),
         name="solve",
-    )(packed, received)
-
-
-def unpack_body(t_ref, out_ref):
+    )(packed, first, second)
+
+
+def unpack_body(turn_ref, t_ref, out_ref, held_ref, sems):
+    turn = turn_ref[0]
+    copies_out = []
     for plane in range(2):
         for comp in range(3):
             lines = [None] * 16
             for half in range(2):
-                slot = slot_of(plane, comp, half)
-                lines[half::2] = swap_blocks([t_ref[chunk, slot] for chunk in range(8)])
-            first = (comp * 2 + plane) * 16
-            out_ref[:, first : first + 16, :] = jnp.swapaxes(jnp.stack(lines), 0, 1)
-
-
-def unpack(received):
+                slot = plane * 6 + slot_of(comp, half)
+                lines[half::2] = swap_blocks([t_ref[turned(chunk, turn), slot] for chunk in range(8)])
+            part = plane * 3 + comp
+            held_ref[part] = jnp.swapaxes(jnp.stack(lines), 0, 1)
+            rows = pl.ds((comp * 2 + plane) * 16, 16)
+            copies_out.append(
+                pltpu.make_async_copy(held_ref.at[part], out_ref.at[:, rows, :], sems.at[part])
+            )
+            copies_out[part].start()
+    for copy in copies_out:
+        copy.wait()
+
+
+def unpack(turn, received):
     return pl.pallas_call(
         unpack_body,
         out_shape=jax.ShapeDtypeStruct((24, 96, 128), F32),
-        in_specs=[pl.BlockSpec(memory_space=VMEM)],
-        out_specs=pl.BlockSpec(memory_space=VMEM),
+        in_specs=[pl.BlockSpec(memory_space=pltpu.SMEM), pl.BlockSpec(memory_space=VMEM)],
+        out_specs=pl.BlockSpec(memory_space=pl.ANY),
+        scratch_shapes=[VMEM((6, 24, 16, 128), F32), pltpu.SemaphoreType.DMA((6,))],
+        compiler_params=pltpu.CompilerParams(vmem_limit_bytes=12 * 2**20),
         name="unpack",
-    )(received)
+    )(turn, received)
 
 
 def exchange(value, axes):
@@ -352,25 +385,36 @@
     planes, width_y, width_z = basis.shape[2:]
     own = width_z // chunks
     scale = 1.0 / (3.0 * planes * width_y * width_z * slabs)
-    density = lax.dynamic_slice_in_dim(density, lax.axis_index(MODE) * own, own, axis=2)
+    turn = lax.axis_index("yh")
+    chunk = lax.axis_index("x") * 2 + lax.abs(lax.axis_index("yl") - turn)
+    density = lax.dynamic_slice_in_dim(density, chunk * own, own, axis=2)
+    turn = turn.reshape(1)
     density = jnp.swapaxes(density.reshape(planes, width_y // 2, 2, own), 1, 2)
     density = density.reshape(planes, 2, width_y // 2 * own)
     root = jnp.sqrt(density)
     weights = jnp.stack([root, density * root])
 
-    near = exchange(pack(basis), MODE)
-    far = lax.ppermute(near[:, 6:], SPACE, [(i, i - 1) for i in range(1, slabs)])
-    part = gram(0, near, near, weights, scale)
-    part = gram(1, near, far, weights, scale, (part,))
-
-    plane_axes, line_axes = MODE + ("yh",), ("zc",)
-    first, last = lax.axis_size(plane_axes), lax.axis_size(line_axes)
-    piece = exchange(part.reshape(first, 384 // first, 128), plane_axes).sum(0)
-    piece = exchange(copies(piece, last), line_axes).sum(0)
-    packed = exchange(copies(piece, first), plane_axes)
-
-    send, inverse, stiff = solve(packed, near)
-    rotated = unpack(exchange(send, MODE)).reshape(basis.shape)
+    first, second = pack(turn, basis)
+    first, second = exchange(first, MODE), exchange(second, MODE)
+    half = slabs // lax.axis_size("yh")
+    route = [
+        (mode * slabs + slab, (mode ^ (slab % half == 0)) * slabs + slab - 1)
+        for mode in range(chunks)
+        for slab in range(1, slabs)
+    ]
+    above = lax.ppermute(first, MODE + SPACE, route)
+    part = gram(0, first, second, first, weights, scale)
+    part = gram(1, second, above, first, weights, scale, (part,))
+
+    plane_axes = MODE + ("yh",)
+    wide, deep = lax.axis_size(plane_axes), lax.axis_size("z")
+    piece = exchange(part.reshape(wide, 384 // wide, 128), plane_axes).sum(0)
+    piece = exchange(copies(piece, deep), "z").sum(0)
+    piece = piece + lax.ppermute(piece, "core", [(0, 1), (1, 0)])
+    packed = exchange(copies(piece, wide), plane_axes)
+
+    send, inverse, stiff = solve(packed, first, second)
+    rotated = unpack(turn, exchange(send, MODE)).reshape(basis.shape)
     high = lax.Precision.HIGHEST
     reduced = jnp.dot(jnp.dot(inverse, stiff, precision=high), inverse.T, precision=high)
     return rotated, reduced
@@ -379,7 +423,7 @@
 def solution(mesh):
     modes, slabs = mesh.devices.shape
     half = 2 if slabs % 4 == 0 else 1
-    inner = Mesh(mesh.devices.reshape(modes // 2, 2, half, slabs // half), MODE + SPACE)
+    inner = Mesh(mesh.devices.reshape(modes // 2, 2, half, slabs // half // 2, 2), MODE + SPACE)
     field = P(MODE, None, SPACE, None, None)
     return jax.shard_map(
         per_device,

time: 124 us -> 118 us (0.952)
  waiting for transfers between devices: 31.7 us -> 22 us
  blocking collectives: 48.2 us -> 57.4 us
  Pallas kernels: 27 us -> 23.4 us
  starting transfers between devices: 12 us -> 10.6 us
    all_to_all x2, waiting for transfers between devices: 31.7 us -> 20.8 us  [exchange(): return lax.all_to_all(value, axes, 0, 0)]
    all_to_all x3 -> x4, blocking collectives: 48.2 us -> 57.4 us  [exchange(): return lax.all_to_all(value, axes, 0, 0)]
    pallas_call x1, Pallas kernels: 3.55 us -> 1.96 us  [unpack(): pl.pallas_call(unpack_body, out_shape=jax.ShapeDtypeStruct((24, 96, 128),...]
    all_to_all x2, starting transfers between devices: 10.7 us -> 9.27 us  [exchange(): return lax.all_to_all(value, axes, 0, 0)]
    pallas_call x1, Pallas kernels: 3.94 us -> 2.54 us  [pack(): pl.pallas_call(pack_body, out_shape=(jax.ShapeDtypeStruct((8, 7, 24, 128)...]
  transfers between devices with their start and end apart: 3 -> 4, of which waited for: 2 -> 3; matrix products, arithmetic and copies ran while one was open for 1% -> 1% of each run, Pallas kernels for 4% -> 5%
where the time goes in v3:
time: 118 us; the launch traced here: 117 us
  blocking collectives  57.4 us (49%)
  Pallas kernels  23.4 us (20%)
  waiting for transfers between devices  22 us (19%)
  starting transfers between devices  10.6 us (9%)
  local copies, waits for them, and re-layouts  1.46 us (1%)
  matrix products  1.34 us (1%)
    all_to_all x4, blocking collectives, exchange(): return lax.all_to_all(value, axes, 0, 0)  57.4 us
    all_to_all x2, waiting for transfers between devices, exchange(): return lax.all_to_all(value, axes, 0, 0)  20.8 us
    pallas_call x2, Pallas kernels, gram(): pl.pallas_call(functools.partial(gram_body, scale, layer), out_shape=jax....  10.8 us
    all_to_all x2, starting transfers between devices, exchange(): return lax.all_to_all(value, axes, 0, 0)  9.27 us
    pallas_call x1, Pallas kernels, solve(): pl.pallas_call(solve_body, out_shape=(jax.ShapeDtypeStruct((8, 12, 24, 12...  8.16 us
    pallas_call x1, Pallas kernels, pack(): pl.pallas_call(pack_body, out_shape=(jax.ShapeDtypeStruct((8, 7, 24, 128)...  2.54 us
  transfers between devices with their start and end apart: 4, of which 3 were waited for; matrix products, arithmetic and copies ran while one was open for 1% of the time, Pallas kernels for 5%

profile of v3, /device:TPU:8, one launch (start us, length us, event | category | flops | bytes accessed | tf_op | source)
XLA Modules:
  0.0 117.2 jit_solution(9548359285991173176)
XLA Ops:
  0.6 0.0 copy-start
  0.7 0.0 copy-start.1
  0.7 1.3 %copy-done.1 = f32[24,3,2,16,128]{4,3,2,1,0:T(8,128)S(1)} copy-done((f32[24,3,2,16,128]{4,3,2,1,0:T(8,128)S(1)}, f32[24,3,2,16,128]{4,3,2,1,0:T(8,128)}, u32[]{:S(2)}) %copy-start.1) | copy-done | bytes 1179672
  1.9 2.5 %pack.1 = (f32[8,7,24,128]{3,2,1,0:T(8,128)S(1)}, f32[8,6,24,128]{3,2,1,0:T(8,128)}) custom-call(s32[1]{0:T(128)} %bitcast.turn_ref, f32[24,96,128]{2,1,0:T(8,128)S(1)} %bitcast.13), custom_call_target="tpu_custom_call" | custom-call | tf_op jit(solution)/shard_map/pack/pallas_call | solution.py:122
  4.5 16.3 %all_to_all.30.first_ref.edge_ref.r0_ref = f32[8,7,24,128]{3,2,1,0:T(8,128)S(1)} all-to-all(f32[8,7,24,128]{3,2,1,0:T(8,128)S(1)} %get-tuple-element.8), channel_id=1, replica_groups=mesh['x'=4,'yl'=2,'yh'=2,'z'=8,'core'=2] {'x','yl'}, dimensions={0} | all-to-all | bytes 1376256 | tf_op jit(solution)/shard_map/all_to_all | solution.py:375
  20.7 4.3 %all-to-all-start = ((f32[8,6,24,128]{3,2,1,0:T(8,128)}), f32[8,6,24,128]{3,2,1,0:T(8,128)S(1)}, u32[]{:S(2)}, u32[]{:S(2)}) async-start(f32[8,6,24,128]{3,2,1,0:T(8,128)} %get-tuple-element.7), calls=%async_computation | async-start | bytes 1179648 | tf_op jit(solution)/shard_map/all_to_all | solution.py:375
  25.1 1.3 %collective-permute-start = (f32[8,7,24,128]{3,2,1,0:T(8,128)S(1)}, f32[8,7,24,128]{3,2,1,0:T(8,128)S(1)}, u32[]{:S(2)}, u32[]{:S(2)}) collective-permute-start(f32[8,7,24,128]{3,2,1,0:T(8,128)S(1)} %all_to_all.30.first_ref.edge_ref.r0_ref), channel_id=1, source_target_pairs={{1,0},{2,1},{3,2},{4,3},{5,4},{6,5},{7,6},{8,7},{9,8},{10,9},{11,1... | collective-permute-start | bytes 2064392 | tf_op jit(solution)/shard_map/ppermute | solution.py:405
  26.4 0.0 copy-done
  26.4 0.1 constant_dynamic-slice_fusion
  26.4 0.1 reshape.50
  26.6 6.9 %all-to-all-done.second_ref.first_ref.r1_ref = f32[8,6,24,128]{3,2,1,0:T(8,128)S(1)} async-done(((f32[8,6,24,128]{3,2,1,0:T(8,128)}), f32[8,6,24,128]{3,2,1,0:T(8,128)S(1)}, u32[]{:S(2)}, u32[]{:S(2)}) %all-to-all-start) | async-done | bytes 589856 | tf_op jit(solution)/shard_map/all_to_all | solution.py:375
  33.4 5.4 %gram.2.rest_0_ = f32[384,128]{1,0:T(8,128)S(1)} custom-call(f32[8,7,24,128]{3,2,1,0:T(8,128)S(1)} %all_to_all.30.first_ref.edge_ref.r0_ref, f32[8,6,24,128]{3,2,1,0:T(8,128)S(1)} %all-to-all-done.second_ref.first_ref.r1_ref, f32[8,7,24,128]{3,2,1,0:T(8,128)S(1)} %all_to_all.30.first_ref.edge_ref.r0_ref, f32[2,2,2,128]{3,2,1,0:T(2,128)S(1)} %pad_maximum_fusion.w_ref), custom_call_target="tpu_custom_call" | custom-call | flops 3000000000 | bytes 3000000 | tf_op jit(solution)/shard_map/gram/pallas_call | solution.py:225
  38.8 0.0 collective-permute-done.second_ref
  38.8 5.4 %gram.3 = f32[384,128]{1,0:T(8,128)S(1)} custom-call(f32[8,6,24,128]{3,2,1,0:T(8,128)S(1)} %all-to-all-done.second_ref.first_ref.r1_ref, f32[8,7,24,128]{3,2,1,0:T(8,128)S(1)} %collective-permute-done.second_ref, f32[8,7,24,128]{3,2,1,0:T(8,128)S(1)} %all_to_all.30.first_ref.edge_ref.r0_ref, f32[2,2,2,128]{3,2,1,0:T(2,128)S(1)} %pad_maximum_fusion.w_ref, ...), custom_call_target="tpu_custom_call" | custom-call | flops 3000000000 | bytes 3000000 | tf_op jit(solution)/shard_map/gram/pallas_call | solution.py:225
  44.2 14.2 %all_to_all.31 = f32[16,24,128]{2,1,0:T(8,128)S(1)} all-to-all(f32[16,24,128]{2,1,0:T(8,128)S(1)} %bitcast.14), channel_id=1, replica_groups=mesh['x'=4,'yl'=2,'yh'=2,'z'=8,'core'=2] {'x','yl','yh'}, dimensions={0} | all-to-all | bytes 393216 | tf_op jit(solution)/shard_map/all_to_all | solution.py:375
  58.5 15.3 %all_to_all.32 = f32[8,24,128]{2,1,0:T(8,128)S(1)} all-to-all(f32[8,24,128]{2,1,0:T(8,128)S(1)} %broadcast_in_dim.4), channel_id=1, replica_groups=mesh['x'=4,'yl'=2,'yh'=2,'z'=8,'core'=2] {'z'}, dimensions={0} | all-to-all | bytes 196608 | tf_op jit(solution)/shard_map/all_to_all | solution.py:375
  73.8 0.1 collective-permute-start.1
  73.9 1.2 collective-permute-done.1
  75.1 11.6 %all_to_all.33.g_ref = f32[16,24,128]{2,1,0:T(8,128)S(1)} all-to-all(f32[16,24,128]{2,1,0:T(8,128)S(1)} %broadcast_in_dim.5), channel_id=1, replica_groups=mesh['x'=4,'yl'=2,'yh'=2,'z'=8,'core'=2] {'x','yl','yh'}, dimensions={0} | all-to-all | bytes 393216 | tf_op jit(solution)/shard_map/all_to_all | solution.py:375
  86.7 8.2 %solve.1 = (f32[8,12,24,128]{3,2,1,0:T(8,128)}, f32[192,192]{1,0:T(8,128)S(1)}, f32[192,192]{1,0:T(8,128)S(1)}) custom-call(f32[16,24,128]{2,1,0:T(8,128)S(1)} %all_to_all.33.g_ref, f32[8,7,24,128]{3,2,1,0:T(8,128)S(1)} %all_to_all.30.first_ref.edge_ref.r0_ref, f32[8,6,24,128]{3,2,1,0:T(8,128)S(1)} %all-to-all-done.second_ref.first_ref.r1_ref), custom_call_target="tpu_custom_call" | custom-call | tf_op jit(solution)/shard_map/solve/pallas_call | solution.py:328
  94.9 4.9 %all-to-all-start.5 = ((f32[8,12,24,128]{3,2,1,0:T(8,128)}), f32[8,12,24,128]{3,2,1,0:T(8,128)S(1)}, u32[]{:S(2)}, u32[]{:S(2)}) async-start(f32[8,12,24,128]{3,2,1,0:T(8,128)} %get-tuple-element.9), calls=%async_computation.5 | async-start | bytes 2359296 | tf_op jit(solution)/shard_map/all_to_all | solution.py:375
  99.8 0.3 fusion.1
  100.1 1.0 fusion.2
  101.2 13.9 %all-to-all-done.5.t_ref = f32[8,12,24,128]{3,2,1,0:T(8,128)S(1)} async-done(((f32[8,12,24,128]{3,2,1,0:T(8,128)}), f32[8,12,24,128]{3,2,1,0:T(8,128)S(1)}, u32[]{:S(2)}, u32[]{:S(2)}) %all-to-all-start.5) | async-done | bytes 1179680 | tf_op jit(solution)/shard_map/all_to_all | solution.py:375
  115.1 2.0 %unpack.1 = f32[24,96,128]{2,1,0:T(8,128)} custom-call(s32[1]{0:T(128)} %bitcast.turn_ref, f32[8,12,24,128]{3,2,1,0:T(8,128)S(1)} %all-to-all-done.5.t_ref), custom_call_target="tpu_custom_call" | custom-call | tf_op jit(solution)/shard_map/unpack/pallas_call | solution.py:363
  (8 shorter events, 0.1 us)
Async XLA Ops:
  0.6 25.7 %copy-start = (f32[2,16,128]{2,1,0:T(8,128)S(1)}, f32[2,16,128]{2,1,0:T(8,128)}, u32[]{:S(2)}) copy-start(f32[2,16,128]{2,1,0:T(8,128)} %param.3) | copy-start | bytes 49156
  0.7 1.3 %copy-start.1 = (f32[24,3,2,16,128]{4,3,2,1,0:T(8,128)S(1)}, f32[24,3,2,16,128]{4,3,2,1,0:T(8,128)}, u32[]{:S(2)}) copy-start(f32[24,3,2,16,128]{4,3,2,1,0:T(8,128)} %param.2) | copy-start | bytes 3538948
  20.7 12.7 %all-to-all-start = ((f32[8,6,24,128]{3,2,1,0:T(8,128)}), f32[8,6,24,128]{3,2,1,0:T(8,128)S(1)}, u32[]{:S(2)}, u32[]{:S(2)}) async-start(f32[8,6,24,128]{3,2,1,0:T(8,128)} %get-tuple-element.7), calls=%async_computation | async-start | bytes 1179648 | tf_op jit(solution)/shard_map/all_to_all | solution.py:375
  25.1 13.7 %collective-permute-start = (f32[8,7,24,128]{3,2,1,0:T(8,128)S(1)}, f32[8,7,24,128]{3,2,1,0:T(8,128)S(1)}, u32[]{:S(2)}, u32[]{:S(2)}) collective-permute-start(f32[8,7,24,128]{3,2,1,0:T(8,128)S(1)} %all_to_all.30.first_ref.edge_ref.r0_ref), channel_id=1, source_target_pairs={{1,0},{2,1},{3,2},{4,3},{5,4},{6,5},{7,6},{8,7},{9,8},{10,9},{11,1... | collective-permute-start | bytes 2064392 | tf_op jit(solution)/shard_map/ppermute | solution.py:405
  73.8 1.3 %collective-permute-start.1 = (f32[24,128]{1,0:T(8,128)S(1)}, f32[24,128]{1,0:T(8,128)S(1)}, u32[]{:S(2)}, u32[]{:S(2)}) collective-permute-start(f32[24,128]{1,0:T(8,128)S(1)} %reduce_sum.19), channel_id=1, source_target_pairs={{0,1},{1,0},{2,3},{3,2},{4,5},{5,4},{6,7},{7,6},{8,9},{9,8},{10,11... | collective-permute-start | bytes 36872 | tf_op jit(solution)/shard_map/ppermute | solution.py:413
  94.9 20.2 %all-to-all-start.5 = ((f32[8,12,24,128]{3,2,1,0:T(8,128)}), f32[8,12,24,128]{3,2,1,0:T(8,128)S(1)}, u32[]{:S(2)}, u32[]{:S(2)}) async-start(f32[8,12,24,128]{3,2,1,0:T(8,128)} %get-tuple-element.9), calls=%async_computation.5 | async-start | bytes 2359296 | tf_op jit(solution)/shard_map/all_to_all | solution.py:375

commit v4 on v3

--- a/solution.py
+++ b/solution.py
@@ -95,50 +95,80 @@
     return chunk + turn if chunk % 2 == 0 else chunk - turn
 
 
-def pack_body(turn_ref, x_ref, out0_ref, out1_ref):
-    outs = (out0_ref, out1_ref)
+def place_lines(lines, comp, turn, out_ref):
+    for half in range(2):
+        parts = swap_blocks([lines[2 * k + half] for k in range(8)])
+        for chunk in range(8):
+            out_ref[turned(chunk, turn), slot_of(comp, half)] = parts[chunk]
+
+
+def pack_first_body(turn_ref, x_ref, out_ref, held_ref, sems):
     turn = turn_ref[0]
+    copies_in = []
+    for part in range(6):
+        rows = pl.ds((part % 3 * 2 + part // 3) * 16, 16)
+        copies_in.append(
+            pltpu.make_async_copy(x_ref.at[:, rows, :], held_ref.at[part], sems.at[part])
+        )
+        copies_in[part].start()
+    within = lax.broadcasted_iota(jnp.int32, (24, 128), 1) % 16
+    edges = [jnp.zeros((24, 128), F32)] * 8
     for plane in range(2):
         for comp in range(3):
-            first = (comp * 2 + plane) * 16
-            lines = jnp.swapaxes(x_ref[:, first : first + 16, :], 0, 1)
+            copies_in[plane * 3 + comp].wait()
+            lines = jnp.swapaxes(held_ref[plane * 3 + comp], 0, 1)
             for half in range(2):
-                parts = swap_blocks([lines[2 * k + half] for k in range(8)])
-                for chunk in range(8):
-                    outs[plane][turned(chunk, turn), slot_of(comp, half)] = parts[chunk]
-    within = lax.broadcasted_iota(jnp.int32, (24, 128), 1) % 16
+                lane = edge_lane(plane, comp, half)
+                for k in range(8):
+                    value = lines[2 * k + half]
+                    value = pltpu.roll(value, lane, 1) if lane else value
+                    edges[k] = jnp.where(within == lane, value, edges[k])
+            if plane == 0:
+                place_lines(lines, comp, turn, out_ref)
+    edges = swap_blocks(edges)
     for chunk in range(8):
-        edge = jnp.zeros((24, 128), F32)
-        for plane in range(2):
-            for comp in range(3):
-                for half in range(2):
-                    lane = edge_lane(plane, comp, half)
-                    value = outs[plane][turned((chunk + 1) % 8, turn), slot_of(comp, half)]
-                    edge = jnp.where(within == lane, pltpu.roll(value, lane, 1), edge)
-        out0_ref[turned(chunk, turn), 6] = edge
-
-
-def pack(turn, basis):
+        out_ref[turned(chunk, turn), 6] = edges[(chunk + 1) % 8]
+
+
+def pack_first(turn, basis):
     return pl.pallas_call(
-        pack_body,
-        out_shape=(
-            jax.ShapeDtypeStruct((8, 7, 24, 128), F32),
-            jax.ShapeDtypeStruct((8, 6, 24, 128), F32),
-        ),
+        pack_first_body,
+        out_shape=jax.ShapeDtypeStruct((8, 7, 24, 128), F32),
+        in_specs=[pl.BlockSpec(memory_space=pltpu.SMEM), pl.BlockSpec(memory_space=pl.ANY)],
+        out_specs=pl.BlockSpec(memory_space=VMEM),
+        scratch_shapes=[VMEM((6, 24, 16, 128), F32), pltpu.SemaphoreType.DMA((6,))],
+        compiler_params=pltpu.CompilerParams(vmem_limit_bytes=60 * 2**20),
+        name="pack_first",
+    )(turn, basis.reshape(24, 96, 128))
+
+
+def pack_second_body(turn_ref, x_ref, out_ref):
+    for comp in range(3):
+        first = (comp * 2 + 1) * 16
+        lines = jnp.swapaxes(x_ref[:, first : first + 16, :], 0, 1)
+        place_lines(lines, comp, turn_ref[0], out_ref)
+
+
+def pack_second(turn, basis):
+    return pl.pallas_call(
+        pack_second_body,
+        out_shape=jax.ShapeDtypeStruct((8, 6, 24, 128), F32),
         in_specs=[pl.BlockSpec(memory_space=pltpu.SMEM), pl.BlockSpec(memory_space=VMEM)],
-        out_specs=[pl.BlockSpec(memory_space=VMEM)] * 2,
+        out_specs=pl.BlockSpec(memory_space=VMEM),
         compiler_params=pltpu.CompilerParams(vmem_limit_bytes=12 * 2**20),
-        name="pack",
+        name="pack_second",
     )(turn, basis.reshape(24, 96, 128))
 
 
-def gram_body(scale, layer, first_ref, second_ref, edge_ref, w_ref, *rest):
+def gram_body(scale, layer, first_ref, second_ref, w_ref, *rest):
     if layer == 0:
-        before_ref, (out_ref, mass_ref, stiff_ref) = None, rest
-        places = ((first_ref, first_ref, 0), (second_ref, first_ref, 1))
+        before_ref = None
+        out_ref, faces_ref, mass_ref, stiff_ref = rest
+        places = ((0, first_ref, first_ref, 0), (1, second_ref, first_ref, 1))
     else:
         before_ref, out_ref, mass_ref, stiff_ref = rest
-        places = ((first_ref, edge_ref, 1), (second_ref, second_ref, 0))
+        faces_ref = first_ref
+        places = ((1, second_ref, second_ref, 0),)
     mass_weight, stiff_rows = factors()
     columns = 192
     last = lax.broadcasted_iota(jnp.int32, (16, 128), 1) % 16 == 15
@@ -153,10 +183,11 @@
     def step(q, carry):
         for g in range(3):
             modes = {}
-            edges = [read(edge, q, g, 6) for _, edge, _ in places]
+            start = pl.multiple_of(q * 48 + g * 16, 16)
+            edges = {a: read(edge, q, g, 6) for a, _, edge, _ in places}
             for comp in range(3):
                 faces = {}
-                for a, (ref, _, plane) in enumerate(places):
+                for a, ref, _, plane in places:
                     lines = {}
                     for half in range(2):
                         here = read(ref, q, g, slot_of(comp, half))
@@ -174,11 +205,17 @@
                 for half in range(2):
                     for pb in range(2):
                         for pc in range(2):
+                            slot = (half * 4 + pb * 2 + pc) * 3 + comp
+                            if layer == 0:
+                                faces_ref[slot, pl.ds(start, 16), :] = faces[1, half, pb, pc]
+                            else:
+                                faces[0, half, pb, pc] = faces_ref[slot, pl.ds(start, 16), :]
+                for half in range(2):
+                    for pb in range(2):
+                        for pc in range(2):
                             low, high = faces[0, half, pb, pc], faces[1, half, pb, pc]
                             modes[half, (2 * pb + pc) * 3 + comp] = high + low
                             modes[half, (4 + 2 * pb + pc) * 3 + comp] = high - low
-            start = pl.multiple_of(q * 48 + g * 16, 16)
-
             def put(ref, slot, value):
                 high = value.astype(BF16)
                 low = (value - high.astype(F32)).astype(BF16)
@@ -201,18 +238,20 @@
 
     lax.fori_loop(0, 4, step, 0)
 
-    def whole(ref):
+    def halves(ref):
         both = lax.dot_general(
             ref[...], ref[:columns, :], (((1,), (1,)), ((), ())), preferred_element_type=F32
         )
-        cross = both[columns:, :]
-        return (both[:columns, :] + cross + cross.T) * scale
-
-    mass, stiff = whole(mass_ref), whole(stiff_ref)
+        return both[:columns, :] + both[columns:, :], both[columns:, :]
+
+    mass, mass_cross = halves(mass_ref)
+    stiff, stiff_cross = halves(stiff_ref)
     row = lax.broadcasted_iota(jnp.int32, (columns, columns), 0)
     col = lax.broadcasted_iota(jnp.int32, (columns, columns), 1)
-    mixed = jnp.where(row >= col, stiff, mass)
-    diagonal = jnp.sum(jnp.where(row == col, mass, 0.0), axis=1, keepdims=True)
+    cross = jnp.where(row <= col, stiff_cross, mass_cross)
+    mixed = (jnp.where(row >= col, stiff, mass) + cross.T) * scale
+    diagonal = jnp.where(row == col, mass + mass_cross, 0.0)
+    diagonal = jnp.sum(diagonal, axis=1, keepdims=True) * scale
     out_ref[:columns, :] = mixed[:, :128]
     out_ref[columns:, :64] = mixed[:, 128:]
     out_ref[columns:, 64:] = jnp.broadcast_to(diagonal, (columns, 64))
@@ -220,13 +259,16 @@
         out_ref[...] += before_ref[...]
 
 
-def gram(layer, first, second, edge, weights, scale, before=()):
+def gram(layer, scale, operands):
     stiff = len(factors()[1])
+    shapes = [jax.ShapeDtypeStruct((384, 128), F32)]
+    if layer == 0:
+        shapes.append(jax.ShapeDtypeStruct((24, 192, 128), F32))
     return pl.pallas_call(
         functools.partial(gram_body, scale, layer),
-        out_shape=jax.ShapeDtypeStruct((384, 128), F32),
-        in_specs=[pl.BlockSpec(memory_space=VMEM)] * (4 + len(before)),
-        out_specs=pl.BlockSpec(memory_space=VMEM),
+        out_shape=shapes,
+        in_specs=[pl.BlockSpec(memory_space=VMEM)] * len(operands),
+        out_specs=[pl.BlockSpec(memory_space=VMEM)] * len(shapes),
         scratch_shapes=[
             VMEM((384, 2 * 24 * 128), BF16),
             VMEM((384, 2 * stiff * 128), BF16),
@@ -234,7 +276,7 @@
         compiler_params=pltpu.CompilerParams(vmem_limit_bytes=20 * 2**20),
         cost_estimate=pl.CostEstimate(flops=3 * 10**9, bytes_accessed=3 * 10**6, transcendentals=0),
         name="gram",
-    )(first, second, edge, weights, *before)
+    )(*operands)
 
 
 def dot32(a, b, contract=((1,), (0,))):
@@ -250,7 +292,11 @@
     spread = {}
     for k in range(size):
         for t in range(k // 8, groups):
-            spread[k, t] = jnp.broadcast_to(block[8 * t : 8 * t + 8, first + k : first + k + 1], (8, 128))
+            tile = (first + k) // 128 * 128
+            index = jnp.full((8, 128), first + k - tile, jnp.int32)
+            spread[k, t] = jnp.take_along_axis(
+                block[8 * t : 8 * t + 8, tile : tile + 128], index, axis=1
+            )
     right = [jnp.where(lane == sub + 8 * t, 1.0, 0.0).astype(F32) for t in range(groups)]
     for i in range(size):
         at, inner = i // 8, i % 8
@@ -278,7 +324,7 @@
     return high, (value - high.astype(F32)).astype(BF16)
 
 
-def solve_body(g_ref, r0_ref, r1_ref, send_ref, inverse_ref, stiff_ref):
+def solve_body(g_ref, r0_ref, r1_ref, send_ref, inverse_ref):
     columns, size = 192, 32
     packed = g_ref[...].reshape(384, 128)
     mixed = jnp.concatenate([packed[:columns], packed[columns:, :64]], axis=1)
@@ -286,10 +332,10 @@
     row = lax.broadcasted_iota(jnp.int32, (columns, columns), 0)
     col = lax.broadcasted_iota(jnp.int32, (columns, columns), 1)
     other = mixed.T
-    stiff_ref[...] = jnp.where(row >= col, mixed, other)
     mass = jnp.where(row < col, mixed, jnp.where(row == col, diagonal, other))
     unit = jnp.where(row == col, 1.0, 0.0).astype(F32)
     count = columns // size
+    mass = jnp.concatenate([mass, jnp.zeros((columns, 64), F32)], axis=1)
     left = [mass[k * size : k * size + size] for k in range(count)]
     right = [unit[k * size : k * size + size] for k in range(count)]
     done = []
@@ -330,10 +376,9 @@
         out_shape=(
             jax.ShapeDtypeStruct((8, 12, 24, 128), F32),
             jax.ShapeDtypeStruct((192, 192), F32),
-            jax.ShapeDtypeStruct((192, 192), F32),
         ),
         in_specs=[pl.BlockSpec(memory_space=VMEM)] * 3,
-        out_specs=[pl.BlockSpec(memory_space=VMEM)] * 3,
+        out_specs=[pl.BlockSpec(memory_space=VMEM)] * 2,
         compiler_params=pltpu.CompilerParams(vmem_limit_bytes=20 * 2**20),
         name="solve",
     )(packed, first, second)
@@ -394,8 +439,8 @@
     root = jnp.sqrt(density)
     weights = jnp.stack([root, density * root])
 
-    first, second = pack(turn, basis)
-    first, second = exchange(first, MODE), exchange(second, MODE)
+    first = exchange(pack_first(turn, basis), MODE)
+    second = exchange(pack_second(turn, basis), MODE)
     half = slabs // lax.axis_size("yh")
     route = [
         (mode * slabs + slab, (mode ^ (slab % half == 0)) * slabs + slab - 1)
@@ -403,19 +448,22 @@
         for slab in range(1, slabs)
     ]
     above = lax.ppermute(first, MODE + SPACE, route)
-    part = gram(0, first, second, first, weights, scale)
-    part = gram(1, second, above, first, weights, scale, (part,))
+    part, faces = gram(0, scale, (first, second, weights))
+    (part,) = gram(1, scale, (faces, above, weights, part))
 
     plane_axes = MODE + ("yh",)
     wide, deep = lax.axis_size(plane_axes), lax.axis_size("z")
     piece = exchange(part.reshape(wide, 384 // wide, 128), plane_axes).sum(0)
+    piece = piece + lax.ppermute(piece, "core", [(0, 1), (1, 0)])
     piece = exchange(copies(piece, deep), "z").sum(0)
-    piece = piece + lax.ppermute(piece, "core", [(0, 1), (1, 0)])
     packed = exchange(copies(piece, wide), plane_axes)
 
-    send, inverse, stiff = solve(packed, first, second)
+    send, inverse = solve(packed, first, second)
     rotated = unpack(turn, exchange(send, MODE)).reshape(basis.shape)
     high = lax.Precision.HIGHEST
+    packed = packed.reshape(384, 128)
+    stiff = jnp.concatenate([packed[:192], packed[192:, :64]], axis=1)
+    stiff = jnp.tril(stiff) + jnp.tril(stiff, -1).T
     reduced = jnp.dot(jnp.dot(inverse, stiff, precision=high), inverse.T, precision=high)
     return rotated, reduced
 

time: 118 us -> 116 us (0.983)
  blocking collectives: 57.4 us -> 41.3 us
  waiting for transfers between devices: 22 us -> 30.6 us
  starting transfers between devices: 10.6 us -> 16.1 us
  Pallas kernels: 23.4 us -> 25.1 us
    all_to_all x4 -> x3, blocking collectives: 57.4 us -> 41.3 us  [exchange(): return lax.all_to_all(value, axes, 0, 0)]
    all_to_all x2 -> x3, waiting for transfers between devices: 20.8 us -> 29.5 us  [exchange(): return lax.all_to_all(value, axes, 0, 0)]
    all_to_all x2 -> x3, starting transfers between devices: 9.27 us -> 14.7 us  [exchange(): return lax.all_to_all(value, axes, 0, 0)]
    pallas_call x3 -> x4, Pallas kernels: 13.3 us -> 15.3 us  [the longest x2 10.7 us: gram(): pl.pallas_call(functools.partial(gram_body, scale, layer), out_shape=shap...]
    unnamed x4, local copies, waits for them, and re-layouts: 1.27 us -> 0.01 us
  transfers between devices with their start and end apart: 4 -> 5, of which waited for: 3 -> 4; matrix products, arithmetic and copies ran while one was open for 1% -> 2% of each run, Pallas kernels for 5% -> 6%
where the time goes in v4:
time: 116 us
  blocking collectives  41.3 us (36%)
  waiting for transfers between devices  30.6 us (26%)
  Pallas kernels  25.1 us (22%)
  starting transfers between devices  16.1 us (14%)
  matrix products  1.45 us (1%)
    all_to_all x3, blocking collectives, exchange(): return lax.all_to_all(value, axes, 0, 0)  41.3 us
    all_to_all x3, waiting for transfers between devices, exchange(): return lax.all_to_all(value, axes, 0, 0)  29.5 us
    all_to_all x3, starting transfers between devices, exchange(): return lax.all_to_all(value, axes, 0, 0)  14.7 us
    pallas_call x2, Pallas kernels, gram(): pl.pallas_call(functools.partial(gram_body, scale, layer), out_shape=shap...  10.7 us
    pallas_call x1, Pallas kernels, solve(): pl.pallas_call(solve_body, out_shape=(jax.ShapeDtypeStruct((8, 12, 24, 12...  7.89 us
    pallas_call x1, Pallas kernels, pack_first(): pl.pallas_call(pack_first_body, out_shape=jax.ShapeDtypeStruct((8, 7, 24,...  3.22 us
  transfers between devices with their start and end apart: 5, of which 4 were waited for; matrix products, arithmetic and copies ran while one was open for 2% of the time, Pallas kernels for 6%

profile of v4, /device:TPU:8, one launch (start us, length us, event | category | flops | bytes accessed | tf_op | source)
XLA Modules:
  0.0 115.8 jit_solution(1109420429050667734)
XLA Ops:
  0.6 0.0 copy-start
  0.7 0.0 copy-start.1
  0.7 3.2 %pack_first.1 = f32[8,7,24,128]{3,2,1,0:T(8,128)} custom-call(s32[1]{0:T(128)} %bitcast.turn_ref, f32[24,96,128]{2,1,0:T(8,128)} %bitcast.17), custom_call_target="tpu_custom_call" | custom-call | tf_op jit(solution)/shard_map/pack_first/pallas_call | solution.py:134
  3.9 5.8 %all-to-all-start = ((f32[8,7,24,128]{3,2,1,0:T(8,128)}), f32[8,7,24,128]{3,2,1,0:T(8,128)S(1)}, u32[]{:S(2)}, u32[]{:S(2)}) async-start(f32[8,7,24,128]{3,2,1,0:T(8,128)} %pack_first.1), calls=%async_computation | async-start | bytes 1376256 | tf_op jit(solution)/shard_map/all_to_all | solution.py:420
  9.7 0.0 copy-done.1
  9.7 1.4 %pack_second.1 = f32[8,6,24,128]{3,2,1,0:T(8,128)} custom-call(s32[1]{0:T(128)} %bitcast.turn_ref, f32[24,96,128]{2,1,0:T(8,128)S(1)} %bitcast.18), custom_call_target="tpu_custom_call" | custom-call | tf_op jit(solution)/shard_map/pack_second/pallas_call | solution.py:153
  11.1 9.3 %all-to-all-done.first_ref.r0_ref = f32[8,7,24,128]{3,2,1,0:T(8,128)S(1)} async-done(((f32[8,7,24,128]{3,2,1,0:T(8,128)}), f32[8,7,24,128]{3,2,1,0:T(8,128)S(1)}, u32[]{:S(2)}, u32[]{:S(2)}) %all-to-all-start) | async-done | bytes 688160 | tf_op jit(solution)/shard_map/all_to_all | solution.py:420
  20.3 4.0 %all-to-all-start.1 = ((f32[8,6,24,128]{3,2,1,0:T(8,128)}), f32[8,6,24,128]{3,2,1,0:T(8,128)S(1)}, u32[]{:S(2)}, u32[]{:S(2)}) async-start(f32[8,6,24,128]{3,2,1,0:T(8,128)} %pack_second.1), calls=%async_computation.1 | async-start | bytes 1179648 | tf_op jit(solution)/shard_map/all_to_all | solution.py:420
  24.3 1.3 %collective-permute-start = (f32[8,7,24,128]{3,2,1,0:T(8,128)S(1)}, f32[8,7,24,128]{3,2,1,0:T(8,128)S(1)}, u32[]{:S(2)}, u32[]{:S(2)}) collective-permute-start(f32[8,7,24,128]{3,2,1,0:T(8,128)S(1)} %all-to-all-done.first_ref.r0_ref), channel_id=1, source_target_pairs={{1,0},{2,1},{3,2},{4,3},{5,4},{6,5},{7,6},{8,7},{9,8},{10,9},{11,1... | collective-permute-start | bytes 2064392 | tf_op jit(solution)/shard_map/ppermute | solution.py:450
  25.6 0.0 copy-done
  25.6 0.1 constant_dynamic-slice_fusion
  25.7 0.1 reshape.55
  25.8 7.6 %all-to-all-done.1.second_ref.r1_ref = f32[8,6,24,128]{3,2,1,0:T(8,128)S(1)} async-done(((f32[8,6,24,128]{3,2,1,0:T(8,128)}), f32[8,6,24,128]{3,2,1,0:T(8,128)S(1)}, u32[]{:S(2)}, u32[]{:S(2)}) %all-to-all-start.1) | async-done | bytes 589856 | tf_op jit(solution)/shard_map/all_to_all | solution.py:420
  33.4 5.4 %gram.2 = (f32[384,128]{1,0:T(8,128)S(1)}, f32[24,192,128]{2,1,0:T(8,128)S(1)}) custom-call(f32[8,7,24,128]{3,2,1,0:T(8,128)S(1)} %all-to-all-done.first_ref.r0_ref, f32[8,6,24,128]{3,2,1,0:T(8,128)S(1)} %all-to-all-done.1.second_ref.r1_ref, f32[2,2,2,128]{3,2,1,0:T(2,128)S(1)} %pad_maximum_fusion.1.w_ref), custom_call_target="tpu_custom_call" | custom-call | flops 3000000000 | bytes 3000000 | tf_op jit(solution)/shard_map/gram/pallas_call | solution.py:267
  38.9 0.0 collective-permute-done.second_ref
  38.9 5.2 %gram.3 = f32[384,128]{1,0:T(8,128)S(1)} custom-call(f32[24,192,128]{2,1,0:T(8,128)S(1)} %get-tuple-element.6.first_ref, f32[8,7,24,128]{3,2,1,0:T(8,128)S(1)} %collective-permute-done.second_ref, f32[2,2,2,128]{3,2,1,0:T(2,128)S(1)} %pad_maximum_fusion.1.w_ref, f32[384,128]{1,0:T(8,128)S(1)} %get-tuple-element.7.rest_0_), custom_call_target="tpu_custom_call" | custom-call | flops 3000000000 | bytes 3000000 | tf_op jit(solution)/shard_map/gram/pallas_call | solution.py:267
  44.1 14.2 %all_to_all.30 = f32[16,24,128]{2,1,0:T(8,128)S(1)} all-to-all(f32[16,24,128]{2,1,0:T(8,128)S(1)} %bitcast.20), channel_id=1, replica_groups=mesh['x'=4,'yl'=2,'yh'=2,'z'=8,'core'=2] {'x','yl','yh'}, dimensions={0} | all-to-all | bytes 393216 | tf_op jit(solution)/shard_map/all_to_all | solution.py:420
  58.3 0.1 collective-permute-start.1
  58.4 1.2 %collective-permute-done.1 = f32[24,128]{1,0:T(8,128)S(1)} collective-permute-done((f32[24,128]{1,0:T(8,128)S(1)}, f32[24,128]{1,0:T(8,128)S(1)}, u32[]{:S(2)}, u32[]{:S(2)}) %collective-permute-start.1) | collective-permute-done | bytes 12320 | tf_op jit(solution)/shard_map/ppermute | solution.py:457
  59.6 15.5 %all_to_all.31 = f32[8,24,128]{2,1,0:T(8,128)S(1)} all-to-all(f32[8,24,128]{2,1,0:T(8,128)S(1)} %broadcast_in_dim.8), channel_id=1, replica_groups=mesh['x'=4,'yl'=2,'yh'=2,'z'=8,'core'=2] {'z'}, dimensions={0} | all-to-all | bytes 196608 | tf_op jit(solution)/shard_map/all_to_all | solution.py:420
  75.1 11.6 %all_to_all.32.g_ref = f32[16,24,128]{2,1,0:T(8,128)S(1)} all-to-all(f32[16,24,128]{2,1,0:T(8,128)S(1)} %broadcast_in_dim.10), channel_id=1, replica_groups=mesh['x'=4,'yl'=2,'yh'=2,'z'=8,'core'=2] {'x','yl','yh'}, dimensions={0} | all-to-all | bytes 393216 | tf_op jit(solution)/shard_map/all_to_all | solution.py:420
  86.7 7.9 %solve.1 = (f32[8,12,24,128]{3,2,1,0:T(8,128)}, f32[192,192]{1,0:T(8,128)S(1)}) custom-call(f32[16,24,128]{2,1,0:T(8,128)S(1)} %all_to_all.32.g_ref, f32[8,7,24,128]{3,2,1,0:T(8,128)S(1)} %all-to-all-done.first_ref.r0_ref, f32[8,6,24,128]{3,2,1,0:T(8,128)S(1)} %all-to-all-done.1.second_ref.r1_ref), custom_call_target="tpu_custom_call" | custom-call | tf_op jit(solution)/shard_map/solve/pallas_call | solution.py:374
  94.6 4.9 %all-to-all-start.5 = ((f32[8,12,24,128]{3,2,1,0:T(8,128)}), f32[8,12,24,128]{3,2,1,0:T(8,128)S(1)}, u32[]{:S(2)}, u32[]{:S(2)}) async-start(f32[8,12,24,128]{3,2,1,0:T(8,128)} %get-tuple-element.8), calls=%async_computation.5 | async-start | bytes 2359296 | tf_op jit(solution)/shard_map/all_to_all | solution.py:420
  99.6 0.1 copy.10
  99.7 0.4 fusion
  100.1 1.0 fusion.8
  101.2 12.6 %all-to-all-done.5.t_ref = f32[8,12,24,128]{3,2,1,0:T(8,128)S(1)} async-done(((f32[8,12,24,128]{3,2,1,0:T(8,128)}), f32[8,12,24,128]{3,2,1,0:T(8,128)S(1)}, u32[]{:S(2)}, u32[]{:S(2)}) %all-to-all-start.5) | async-done | bytes 1179680 | tf_op jit(solution)/shard_map/all_to_all | solution.py:420
  113.7 2.0 %unpack.1 = f32[24,96,128]{2,1,0:T(8,128)} custom-call(s32[1]{0:T(128)} %bitcast.turn_ref, f32[8,12,24,128]{3,2,1,0:T(8,128)S(1)} %all-to-all-done.5.t_ref), custom_call_target="tpu_custom_call" | custom-call | tf_op jit(solution)/shard_map/unpack/pallas_call | solution.py:408
  (12 shorter events, 0.1 us)
Async XLA Ops:
  0.6 25.0 %copy-start = (f32[2,16,128]{2,1,0:T(8,128)S(1)}, f32[2,16,128]{2,1,0:T(8,128)}, u32[]{:S(2)}) copy-start(f32[2,16,128]{2,1,0:T(8,128)} %param.3) | copy-start | bytes 49156
  0.7 9.0 %copy-start.1 = (f32[24,3,2,16,128]{4,3,2,1,0:T(8,128)S(1)}, f32[24,3,2,16,128]{4,3,2,1,0:T(8,128)}, u32[]{:S(2)}) copy-start(f32[24,3,2,16,128]{4,3,2,1,0:T(8,128)} %param.2) | copy-start | bytes 3538948
  3.9 16.4 %all-to-all-start = ((f32[8,7,24,128]{3,2,1,0:T(8,128)}), f32[8,7,24,128]{3,2,1,0:T(8,128)S(1)}, u32[]{:S(2)}, u32[]{:S(2)}) async-start(f32[8,7,24,128]{3,2,1,0:T(8,128)} %pack_first.1), calls=%async_computation | async-start | bytes 1376256 | tf_op jit(solution)/shard_map/all_to_all | solution.py:420
  20.3 13.1 %all-to-all-start.1 = ((f32[8,6,24,128]{3,2,1,0:T(8,128)}), f32[8,6,24,128]{3,2,1,0:T(8,128)S(1)}, u32[]{:S(2)}, u32[]{:S(2)}) async-start(f32[8,6,24,128]{3,2,1,0:T(8,128)} %pack_second.1), calls=%async_computation.1 | async-start | bytes 1179648 | tf_op jit(solution)/shard_map/all_to_all | solution.py:420
  24.3 14.5 %collective-permute-start = (f32[8,7,24,128]{3,2,1,0:T(8,128)S(1)}, f32[8,7,24,128]{3,2,1,0:T(8,128)S(1)}, u32[]{:S(2)}, u32[]{:S(2)}) collective-permute-start(f32[8,7,24,128]{3,2,1,0:T(8,128)S(1)} %all-to-all-done.first_ref.r0_ref), channel_id=1, source_target_pairs={{1,0},{2,1},{3,2},{4,3},{5,4},{6,5},{7,6},{8,7},{9,8},{10,9},{11,1... | collective-permute-start | bytes 2064392 | tf_op jit(solution)/shard_map/ppermute | solution.py:450
  58.3 1.3 %collective-permute-start.1 = (f32[24,128]{1,0:T(8,128)S(1)}, f32[24,128]{1,0:T(8,128)S(1)}, u32[]{:S(2)}, u32[]{:S(2)}) collective-permute-start(f32[24,128]{1,0:T(8,128)S(1)} %reduce_sum.18), channel_id=1, source_target_pairs={{0,1},{1,0},{2,3},{3,2},{4,5},{5,4},{6,7},{7,6},{8,9},{9,8},{10,11... | collective-permute-start | bytes 36872 | tf_op jit(solution)/shard_map/ppermute | solution.py:457
  94.6 19.1 %all-to-all-start.5 = ((f32[8,12,24,128]{3,2,1,0:T(8,128)}), f32[8,12,24,128]{3,2,1,0:T(8,128)S(1)}, u32[]{:S(2)}, u32[]{:S(2)}) async-start(f32[8,12,24,128]{3,2,1,0:T(8,128)} %get-tuple-element.8), calls=%async_computation.5 | async-start | bytes 2359296 | tf_op jit(solution)/shard_map/all_to_all | solution.py:420

commit v5 on v4

--- a/solution.py
+++ b/solution.py
@@ -324,7 +324,8 @@
     return high, (value - high.astype(F32)).astype(BF16)
 
 
-def solve_body(g_ref, r0_ref, r1_ref, send_ref, inverse_ref):
+def solve_body(g_ref, r0_ref, r1_ref, send_ref, inverse_ref, held_ref, sems):
+    copies_out = []
     columns, size = 192, 32
     packed = g_ref[...].reshape(384, 128)
     mixed = jnp.concatenate([packed[:columns], packed[columns:, :64]], axis=1)
@@ -367,7 +368,13 @@
             total += jnp.dot(left_low, right_high, preferred_element_type=F32)
             for half in range(2):
                 part = total[:, 128 * half : 128 * half + 128].reshape(8, 24, 128)
-                send_ref[:, plane * 6 + slot_of(comp, half)] = part
+                held_ref[plane * 3 + comp, :, half] = part
+            at = plane * 3 + comp
+            target = send_ref.at[:, pl.ds(2 * at, 2)]
+            copies_out.append(pltpu.make_async_copy(held_ref.at[at], target, sems.at[at]))
+            copies_out[at].start()
+    for copy in copies_out:
+        copy.wait()
 
 
 def solve(packed, first, second):
@@ -378,7 +385,8 @@
             jax.ShapeDtypeStruct((192, 192), F32),
         ),
         in_specs=[pl.BlockSpec(memory_space=VMEM)] * 3,
-        out_specs=[pl.BlockSpec(memory_space=VMEM)] * 2,
+        out_specs=[pl.BlockSpec(memory_space=pl.ANY), pl.BlockSpec(memory_space=VMEM)],
+        scratch_shapes=[VMEM((6, 8, 2, 24, 128), F32), pltpu.SemaphoreType.DMA((6,))],
         compiler_params=pltpu.CompilerParams(vmem_limit_bytes=20 * 2**20),
         name="solve",
     )(packed, first, second)
@@ -451,7 +459,7 @@
     part, faces = gram(0, scale, (first, second, weights))
     (part,) = gram(1, scale, (faces, above, weights, part))
 
-    plane_axes = MODE + ("yh",)
+    plane_axes = ("yh", "yl", "x")
     wide, deep = lax.axis_size(plane_axes), lax.axis_size("z")
     piece = exchange(part.reshape(wide, 384 // wide, 128), plane_axes).sum(0)
     piece = piece + lax.ppermute(piece, "core", [(0, 1), (1, 0)])

time: 116 us -> 116 us (level)
  no operation moved by 1% of the time
where the time goes in v5:
time: 116 us; the launch traced here: 115 us
  blocking collectives  40.3 us (35%)
  waiting for transfers between devices  30.6 us (26%)
  Pallas kernels  24.9 us (21%)
  starting transfers between devices  16.6 us (14%)
  matrix products  1.45 us (1%)
    all_to_all x3, blocking collectives, exchange(): return lax.all_to_all(value, axes, 0, 0)  40.3 us
    all_to_all x3, waiting for transfers between devices, exchange(): return lax.all_to_all(value, axes, 0, 0)  29.5 us
    all_to_all x3, starting transfers between devices, exchange(): return lax.all_to_all(value, axes, 0, 0)  15.2 us
    pallas_call x2, Pallas kernels, gram(): pl.pallas_call(functools.partial(gram_body, scale, layer), out_shape=shap...  10.7 us
    pallas_call x1, Pallas kernels, solve(): pl.pallas_call(solve_body, out_shape=(jax.ShapeDtypeStruct((8, 12, 24, 12...  7.68 us
    pallas_call x1, Pallas kernels, pack_first(): pl.pallas_call(pack_first_body, out_shape=jax.ShapeDtypeStruct((8, 7, 24,...  3.22 us
  transfers between devices with their start and end apart: 5, of which 4 were waited for; matrix products, arithmetic and copies ran while one was open for 2% of the time, Pallas kernels for 6%

profile of v5, /device:TPU:8, one launch (start us, length us, event | category | flops | bytes accessed | tf_op | source)
XLA Modules:
  0.0 115.2 jit_solution(13545810277708428669)
XLA Ops:
  0.6 0.0 copy-start
  0.7 0.0 copy-start.1
  0.7 3.2 %pack_first.1 = f32[8,7,24,128]{3,2,1,0:T(8,128)} custom-call(s32[1]{0:T(128)} %bitcast.turn_ref, f32[24,96,128]{2,1,0:T(8,128)} %bitcast.17), custom_call_target="tpu_custom_call" | custom-call | tf_op jit(solution)/shard_map/pack_first/pallas_call | solution.py:134
  3.9 5.8 %all-to-all-start = ((f32[8,7,24,128]{3,2,1,0:T(8,128)}), f32[8,7,24,128]{3,2,1,0:T(8,128)S(1)}, u32[]{:S(2)}, u32[]{:S(2)}) async-start(f32[8,7,24,128]{3,2,1,0:T(8,128)} %pack_first.1), calls=%async_computation | async-start | bytes 1376256 | tf_op jit(solution)/shard_map/all_to_all | solution.py:428
  9.7 0.0 copy-done.1
  9.7 1.4 %pack_second.1 = f32[8,6,24,128]{3,2,1,0:T(8,128)} custom-call(s32[1]{0:T(128)} %bitcast.turn_ref, f32[24,96,128]{2,1,0:T(8,128)S(1)} %bitcast.18), custom_call_target="tpu_custom_call" | custom-call | tf_op jit(solution)/shard_map/pack_second/pallas_call | solution.py:153
  11.1 9.3 %all-to-all-done.first_ref.r0_ref = f32[8,7,24,128]{3,2,1,0:T(8,128)S(1)} async-done(((f32[8,7,24,128]{3,2,1,0:T(8,128)}), f32[8,7,24,128]{3,2,1,0:T(8,128)S(1)}, u32[]{:S(2)}, u32[]{:S(2)}) %all-to-all-start) | async-done | bytes 688160 | tf_op jit(solution)/shard_map/all_to_all | solution.py:428
  20.3 4.0 %all-to-all-start.1 = ((f32[8,6,24,128]{3,2,1,0:T(8,128)}), f32[8,6,24,128]{3,2,1,0:T(8,128)S(1)}, u32[]{:S(2)}, u32[]{:S(2)}) async-start(f32[8,6,24,128]{3,2,1,0:T(8,128)} %pack_second.1), calls=%async_computation.1 | async-start | bytes 1179648 | tf_op jit(solution)/shard_map/all_to_all | solution.py:428
  24.3 1.3 %collective-permute-start = (f32[8,7,24,128]{3,2,1,0:T(8,128)S(1)}, f32[8,7,24,128]{3,2,1,0:T(8,128)S(1)}, u32[]{:S(2)}, u32[]{:S(2)}) collective-permute-start(f32[8,7,24,128]{3,2,1,0:T(8,128)S(1)} %all-to-all-done.first_ref.r0_ref), channel_id=1, source_target_pairs={{1,0},{2,1},{3,2},{4,3},{5,4},{6,5},{7,6},{8,7},{9,8},{10,9},{11,1... | collective-permute-start | bytes 2064392 | tf_op jit(solution)/shard_map/ppermute | solution.py:458
  25.6 0.0 copy-done
  25.6 0.1 constant_dynamic-slice_fusion
  25.7 0.1 reshape.55
  25.8 7.6 %all-to-all-done.1.second_ref.r1_ref = f32[8,6,24,128]{3,2,1,0:T(8,128)S(1)} async-done(((f32[8,6,24,128]{3,2,1,0:T(8,128)}), f32[8,6,24,128]{3,2,1,0:T(8,128)S(1)}, u32[]{:S(2)}, u32[]{:S(2)}) %all-to-all-start.1) | async-done | bytes 589856 | tf_op jit(solution)/shard_map/all_to_all | solution.py:428
  33.4 5.4 %gram.2 = (f32[384,128]{1,0:T(8,128)S(1)}, f32[24,192,128]{2,1,0:T(8,128)S(1)}) custom-call(f32[8,7,24,128]{3,2,1,0:T(8,128)S(1)} %all-to-all-done.first_ref.r0_ref, f32[8,6,24,128]{3,2,1,0:T(8,128)S(1)} %all-to-all-done.1.second_ref.r1_ref, f32[2,2,2,128]{3,2,1,0:T(2,128)S(1)} %pad_maximum_fusion.1.w_ref), custom_call_target="tpu_custom_call" | custom-call | flops 3000000000 | bytes 3000000 | tf_op jit(solution)/shard_map/gram/pallas_call | solution.py:267
  38.9 0.0 collective-permute-done.second_ref
  38.9 5.2 %gram.3 = f32[384,128]{1,0:T(8,128)S(1)} custom-call(f32[24,192,128]{2,1,0:T(8,128)S(1)} %get-tuple-element.6.first_ref, f32[8,7,24,128]{3,2,1,0:T(8,128)S(1)} %collective-permute-done.second_ref, f32[2,2,2,128]{3,2,1,0:T(2,128)S(1)} %pad_maximum_fusion.1.w_ref, f32[384,128]{1,0:T(8,128)S(1)} %get-tuple-element.7.rest_0_), custom_call_target="tpu_custom_call" | custom-call | flops 3000000000 | bytes 3000000 | tf_op jit(solution)/shard_map/gram/pallas_call | solution.py:267
  44.1 13.5 %all_to_all.30 = f32[16,24,128]{2,1,0:T(8,128)S(1)} all-to-all(f32[16,24,128]{2,1,0:T(8,128)S(1)} %bitcast.20), channel_id=1, replica_groups=mesh['x'=4,'yl'=2,'yh'=2,'z'=8,'core'=2] {'yh','yl','x'}, dimensions={0} | all-to-all | bytes 393216 | tf_op jit(solution)/shard_map/all_to_all | solution.py:428
  57.6 0.1 collective-permute-start.1
  57.7 1.2 %collective-permute-done.1 = f32[24,128]{1,0:T(8,128)S(1)} collective-permute-done((f32[24,128]{1,0:T(8,128)S(1)}, f32[24,128]{1,0:T(8,128)S(1)}, u32[]{:S(2)}, u32[]{:S(2)}) %collective-permute-start.1) | collective-permute-done | bytes 12320 | tf_op jit(solution)/shard_map/ppermute | solution.py:465
  58.9 15.5 %all_to_all.31 = f32[8,24,128]{2,1,0:T(8,128)S(1)} all-to-all(f32[8,24,128]{2,1,0:T(8,128)S(1)} %broadcast_in_dim.8), channel_id=1, replica_groups=mesh['x'=4,'yl'=2,'yh'=2,'z'=8,'core'=2] {'z'}, dimensions={0} | all-to-all | bytes 196608 | tf_op jit(solution)/shard_map/all_to_all | solution.py:428
  74.4 11.3 %all_to_all.32.g_ref = f32[16,24,128]{2,1,0:T(8,128)S(1)} all-to-all(f32[16,24,128]{2,1,0:T(8,128)S(1)} %broadcast_in_dim.10), channel_id=1, replica_groups=mesh['x'=4,'yl'=2,'yh'=2,'z'=8,'core'=2] {'yh','yl','x'}, dimensions={0} | all-to-all | bytes 393216 | tf_op jit(solution)/shard_map/all_to_all | solution.py:428
  85.8 7.7 %solve.1 = (f32[8,12,24,128]{3,2,1,0:T(8,128)}, f32[192,192]{1,0:T(8,128)S(1)}) custom-call(f32[16,24,128]{2,1,0:T(8,128)S(1)} %all_to_all.32.g_ref, f32[8,7,24,128]{3,2,1,0:T(8,128)S(1)} %all-to-all-done.first_ref.r0_ref, f32[8,6,24,128]{3,2,1,0:T(8,128)S(1)} %all-to-all-done.1.second_ref.r1_ref), custom_call_target="tpu_custom_call" | custom-call | tf_op jit(solution)/shard_map/solve/pallas_call | solution.py:381
  93.5 5.5 %all-to-all-start.5 = ((f32[8,12,24,128]{3,2,1,0:T(8,128)}), f32[8,12,24,128]{3,2,1,0:T(8,128)S(1)}, u32[]{:S(2)}, u32[]{:S(2)}) async-start(f32[8,12,24,128]{3,2,1,0:T(8,128)} %get-tuple-element.8), calls=%async_computation.5 | async-start | bytes 2359296 | tf_op jit(solution)/shard_map/all_to_all | solution.py:428
  99.0 0.1 copy.10
  99.1 0.4 fusion
  99.5 1.0 fusion.8
  100.6 12.6 %all-to-all-done.5.t_ref = f32[8,12,24,128]{3,2,1,0:T(8,128)S(1)} async-done(((f32[8,12,24,128]{3,2,1,0:T(8,128)}), f32[8,12,24,128]{3,2,1,0:T(8,128)S(1)}, u32[]{:S(2)}, u32[]{:S(2)}) %all-to-all-start.5) | async-done | bytes 1179680 | tf_op jit(solution)/shard_map/all_to_all | solution.py:428
  113.1 2.0 %unpack.1 = f32[24,96,128]{2,1,0:T(8,128)} custom-call(s32[1]{0:T(128)} %bitcast.turn_ref, f32[8,12,24,128]{3,2,1,0:T(8,128)S(1)} %all-to-all-done.5.t_ref), custom_call_target="tpu_custom_call" | custom-call | tf_op jit(solution)/shard_map/unpack/pallas_call | solution.py:416
  (12 shorter events, 0.1 us)
Async XLA Ops:
  0.6 25.0 %copy-start = (f32[2,16,128]{2,1,0:T(8,128)S(1)}, f32[2,16,128]{2,1,0:T(8,128)}, u32[]{:S(2)}) copy-start(f32[2,16,128]{2,1,0:T(8,128)} %param.3) | copy-start | bytes 49156
  0.7 9.0 %copy-start.1 = (f32[24,3,2,16,128]{4,3,2,1,0:T(8,128)S(1)}, f32[24,3,2,16,128]{4,3,2,1,0:T(8,128)}, u32[]{:S(2)}) copy-start(f32[24,3,2,16,128]{4,3,2,1,0:T(8,128)} %param.2) | copy-start | bytes 3538948
  3.9 16.4 %all-to-all-start = ((f32[8,7,24,128]{3,2,1,0:T(8,128)}), f32[8,7,24,128]{3,2,1,0:T(8,128)S(1)}, u32[]{:S(2)}, u32[]{:S(2)}) async-start(f32[8,7,24,128]{3,2,1,0:T(8,128)} %pack_first.1), calls=%async_computation | async-start | bytes 1376256 | tf_op jit(solution)/shard_map/all_to_all | solution.py:428
  20.3 13.1 %all-to-all-start.1 = ((f32[8,6,24,128]{3,2,1,0:T(8,128)}), f32[8,6,24,128]{3,2,1,0:T(8,128)S(1)}, u32[]{:S(2)}, u32[]{:S(2)}) async-start(f32[8,6,24,128]{3,2,1,0:T(8,128)} %pack_second.1), calls=%async_computation.1 | async-start | bytes 1179648 | tf_op jit(solution)/shard_map/all_to_all | solution.py:428
  24.3 14.5 %collective-permute-start = (f32[8,7,24,128]{3,2,1,0:T(8,128)S(1)}, f32[8,7,24,128]{3,2,1,0:T(8,128)S(1)}, u32[]{:S(2)}, u32[]{:S(2)}) collective-permute-start(f32[8,7,24,128]{3,2,1,0:T(8,128)S(1)} %all-to-all-done.first_ref.r0_ref), channel_id=1, source_target_pairs={{1,0},{2,1},{3,2},{4,3},{5,4},{6,5},{7,6},{8,7},{9,8},{10,9},{11,1... | collective-permute-start | bytes 2064392 | tf_op jit(solution)/shard_map/ppermute | solution.py:458
  57.6 1.3 %collective-permute-start.1 = (f32[24,128]{1,0:T(8,128)S(1)}, f32[24,128]{1,0:T(8,128)S(1)}, u32[]{:S(2)}, u32[]{:S(2)}) collective-permute-start(f32[24,128]{1,0:T(8,128)S(1)} %reduce_sum.18), channel_id=1, source_target_pairs={{0,1},{1,0},{2,3},{3,2},{4,5},{5,4},{6,7},{7,6},{8,9},{9,8},{10,11... | collective-permute-start | bytes 36872 | tf_op jit(solution)/shard_map/ppermute | solution.py:465
  93.5 19.7 %all-to-all-start.5 = ((f32[8,12,24,128]{3,2,1,0:T(8,128)}), f32[8,12,24,128]{3,2,1,0:T(8,128)S(1)}, u32[]{:S(2)}, u32[]{:S(2)}) async-start(f32[8,12,24,128]{3,2,1,0:T(8,128)} %get-tuple-element.8), calls=%async_computation.5 | async-start | bytes 2359296 | tf_op jit(solution)/shard_map/all_to_all | solution.py:428

commit v6 on v5

--- a/solution.py
+++ b/solution.py
@@ -11,6 +11,7 @@
 
 VMEM = pltpu.VMEM
 MODE = ("x", "yl")
+TURNED = ("yl", "x")
 SPACE = ("yh", "z", "core")
 F32 = jnp.float32
 BF16 = jnp.bfloat16
@@ -92,7 +93,7 @@
 
 
 def turned(chunk, turn):
-    return chunk + turn if chunk % 2 == 0 else chunk - turn
+    return chunk // 2 + (4 * turn if chunk % 2 == 0 else 4 - 4 * turn)
 
 
 def place_lines(lines, comp, turn, out_ref):
@@ -177,7 +178,7 @@
         parts = []
         for n in (2 * g, 2 * g + 1):
             t = n % 3
-            parts.append(ref[2 * q + n // 3, slot, 8 * t : 8 * t + 8, :])
+            parts.append(ref[n // 3 * 4 + q, slot, 8 * t : 8 * t + 8, :])
         return jnp.concatenate(parts, axis=0)
 
     def step(q, carry):
@@ -361,14 +362,18 @@
     left_high, left_low = split(inverse)
     for plane, ref in enumerate((r0_ref, r1_ref)):
         for comp in range(3):
-            sides = [ref[:, slot_of(comp, half)].reshape(columns, 128) for half in range(2)]
+            sides = [
+                jnp.concatenate([ref[m % 2 * 4 + m // 2, slot_of(comp, half)] for m in range(8)])
+                for half in range(2)
+            ]
             right_high, right_low = split(jnp.concatenate(sides, axis=1))
             total = jnp.dot(left_high, right_high, preferred_element_type=F32)
             total += jnp.dot(left_high, right_low, preferred_element_type=F32)
             total += jnp.dot(left_low, right_high, preferred_element_type=F32)
             for half in range(2):
                 part = total[:, 128 * half : 128 * half + 128].reshape(8, 24, 128)
-                held_ref[plane * 3 + comp, :, half] = part
+                for m in range(8):
+                    held_ref[plane * 3 + comp, m % 2 * 4 + m // 2, half] = part[m]
             at = plane * 3 + comp
             target = send_ref.at[:, pl.ds(2 * at, 2)]
             copies_out.append(pltpu.make_async_copy(held_ref.at[at], target, sems.at[at]))
@@ -447,8 +452,8 @@
     root = jnp.sqrt(density)
     weights = jnp.stack([root, density * root])
 
-    first = exchange(pack_first(turn, basis), MODE)
-    second = exchange(pack_second(turn, basis), MODE)
+    first = exchange(pack_first(turn, basis), TURNED)
+    second = exchange(pack_second(turn, basis), TURNED)
     half = slabs // lax.axis_size("yh")
     route = [
         (mode * slabs + slab, (mode ^ (slab % half == 0)) * slabs + slab - 1)
@@ -467,7 +472,7 @@
     packed = exchange(copies(piece, wide), plane_axes)
 
     send, inverse = solve(packed, first, second)
-    rotated = unpack(turn, exchange(send, MODE)).reshape(basis.shape)
+    rotated = unpack(turn, exchange(send, TURNED)).reshape(basis.shape)
     high = lax.Precision.HIGHEST
     packed = packed.reshape(384, 128)
     stiff = jnp.concatenate([packed[:192], packed[192:, :64]], axis=1)

time: 116 us -> 117 us (level)
  no operation moved by 1% of the time
where the time goes in v6:
time: 117 us; the launch traced here: 116 us
  blocking collectives  40.7 us (35%)
  waiting for transfers between devices  29.8 us (25%)
  Pallas kernels  25 us (21%)
  starting transfers between devices  17.6 us (15%)
  matrix products  1.45 us (1%)
    all_to_all x3, blocking collectives, exchange(): return lax.all_to_all(value, axes, 0, 0)  40.7 us
    all_to_all x3, waiting for transfers between devices, exchange(): return lax.all_to_all(value, axes, 0, 0)  28.6 us
    all_to_all x3, starting transfers between devices, exchange(): return lax.all_to_all(value, axes, 0, 0)  16.2 us
    pallas_call x2, Pallas kernels, gram(): pl.pallas_call(functools.partial(gram_body, scale, layer), out_shape=shap...  10.7 us
    pallas_call x1, Pallas kernels, solve(): pl.pallas_call(solve_body, out_shape=(jax.ShapeDtypeStruct((8, 12, 24, 12...  7.69 us
    pallas_call x1, Pallas kernels, pack_first(): pl.pallas_call(pack_first_body, out_shape=jax.ShapeDtypeStruct((8, 7, 24,...  3.22 us
  transfers between devices with their start and end apart: 5, of which 4 were waited for; matrix products, arithmetic and copies ran while one was open for 2% of the time, Pallas kernels for 6%

profile of v6, /device:TPU:8, one launch (start us, length us, event | category | flops | bytes accessed | tf_op | source)
XLA Modules:
  0.0 115.8 jit_solution(2740628313438076553)
XLA Ops:
  0.6 0.0 copy-start
  0.7 0.0 copy-start.1
  0.7 3.2 %pack_first.1 = f32[8,7,24,128]{3,2,1,0:T(8,128)} custom-call(s32[1]{0:T(128)} %bitcast.turn_ref, f32[24,96,128]{2,1,0:T(8,128)} %bitcast.17), custom_call_target="tpu_custom_call" | custom-call | tf_op jit(solution)/shard_map/pack_first/pallas_call | solution.py:135
  3.9 5.8 %all-to-all-start = ((f32[8,7,24,128]{3,2,1,0:T(8,128)}), f32[8,7,24,128]{3,2,1,0:T(8,128)S(1)}, u32[]{:S(2)}, u32[]{:S(2)}) async-start(f32[8,7,24,128]{3,2,1,0:T(8,128)} %pack_first.1), calls=%async_computation | async-start | bytes 1376256 | tf_op jit(solution)/shard_map/all_to_all | solution.py:433
  9.7 0.0 copy-done.1
  9.7 1.4 %pack_second.1 = f32[8,6,24,128]{3,2,1,0:T(8,128)} custom-call(s32[1]{0:T(128)} %bitcast.turn_ref, f32[24,96,128]{2,1,0:T(8,128)S(1)} %bitcast.18), custom_call_target="tpu_custom_call" | custom-call | tf_op jit(solution)/shard_map/pack_second/pallas_call | solution.py:154
  11.1 9.0 %all-to-all-done.first_ref.r0_ref = f32[8,7,24,128]{3,2,1,0:T(8,128)S(1)} async-done(((f32[8,7,24,128]{3,2,1,0:T(8,128)}), f32[8,7,24,128]{3,2,1,0:T(8,128)S(1)}, u32[]{:S(2)}, u32[]{:S(2)}) %all-to-all-start) | async-done | bytes 688160 | tf_op jit(solution)/shard_map/all_to_all | solution.py:433
  20.0 4.9 %all-to-all-start.1 = ((f32[8,6,24,128]{3,2,1,0:T(8,128)}), f32[8,6,24,128]{3,2,1,0:T(8,128)S(1)}, u32[]{:S(2)}, u32[]{:S(2)}) async-start(f32[8,6,24,128]{3,2,1,0:T(8,128)} %pack_second.1), calls=%async_computation.1 | async-start | bytes 1179648 | tf_op jit(solution)/shard_map/all_to_all | solution.py:433
  25.0 1.3 %collective-permute-start = (f32[8,7,24,128]{3,2,1,0:T(8,128)S(1)}, f32[8,7,24,128]{3,2,1,0:T(8,128)S(1)}, u32[]{:S(2)}, u32[]{:S(2)}) collective-permute-start(f32[8,7,24,128]{3,2,1,0:T(8,128)S(1)} %all-to-all-done.first_ref.r0_ref), channel_id=1, source_target_pairs={{1,0},{2,1},{3,2},{4,3},{5,4},{6,5},{7,6},{8,7},{9,8},{10,9},{11,1... | collective-permute-start | bytes 2064392 | tf_op jit(solution)/shard_map/ppermute | solution.py:463
  26.3 0.0 copy-done
  26.3 0.1 constant_dynamic-slice_fusion
  26.3 0.1 reshape.55
  26.5 7.9 %all-to-all-done.1.second_ref.r1_ref = f32[8,6,24,128]{3,2,1,0:T(8,128)S(1)} async-done(((f32[8,6,24,128]{3,2,1,0:T(8,128)}), f32[8,6,24,128]{3,2,1,0:T(8,128)S(1)}, u32[]{:S(2)}, u32[]{:S(2)}) %all-to-all-start.1) | async-done | bytes 589856 | tf_op jit(solution)/shard_map/all_to_all | solution.py:433
  34.4 5.5 %gram.2 = (f32[384,128]{1,0:T(8,128)S(1)}, f32[24,192,128]{2,1,0:T(8,128)S(1)}) custom-call(f32[8,7,24,128]{3,2,1,0:T(8,128)S(1)} %all-to-all-done.first_ref.r0_ref, f32[8,6,24,128]{3,2,1,0:T(8,128)S(1)} %all-to-all-done.1.second_ref.r1_ref, f32[2,2,2,128]{3,2,1,0:T(2,128)S(1)} %pad_maximum_fusion.1.w_ref), custom_call_target="tpu_custom_call" | custom-call | flops 3000000000 | bytes 3000000 | tf_op jit(solution)/shard_map/gram/pallas_call | solution.py:268
  39.9 0.0 collective-permute-done.second_ref
  39.9 5.2 %gram.3 = f32[384,128]{1,0:T(8,128)S(1)} custom-call(f32[24,192,128]{2,1,0:T(8,128)S(1)} %get-tuple-element.6.first_ref, f32[8,7,24,128]{3,2,1,0:T(8,128)S(1)} %collective-permute-done.second_ref, f32[2,2,2,128]{3,2,1,0:T(2,128)S(1)} %pad_maximum_fusion.1.w_ref, f32[384,128]{1,0:T(8,128)S(1)} %get-tuple-element.7.rest_0_), custom_call_target="tpu_custom_call" | custom-call | flops 3000000000 | bytes 3000000 | tf_op jit(solution)/shard_map/gram/pallas_call | solution.py:268
  45.1 13.8 %all_to_all.30 = f32[16,24,128]{2,1,0:T(8,128)S(1)} all-to-all(f32[16,24,128]{2,1,0:T(8,128)S(1)} %bitcast.20), channel_id=1, replica_groups=mesh['x'=4,'yl'=2,'yh'=2,'z'=8,'core'=2] {'yh','yl','x'}, dimensions={0} | all-to-all | bytes 393216 | tf_op jit(solution)/shard_map/all_to_all | solution.py:433
  58.9 0.1 collective-permute-start.1
  59.0 1.2 %collective-permute-done.1 = f32[24,128]{1,0:T(8,128)S(1)} collective-permute-done((f32[24,128]{1,0:T(8,128)S(1)}, f32[24,128]{1,0:T(8,128)S(1)}, u32[]{:S(2)}, u32[]{:S(2)}) %collective-permute-start.1) | collective-permute-done | bytes 12320 | tf_op jit(solution)/shard_map/ppermute | solution.py:470
  60.2 15.5 %all_to_all.31 = f32[8,24,128]{2,1,0:T(8,128)S(1)} all-to-all(f32[8,24,128]{2,1,0:T(8,128)S(1)} %broadcast_in_dim.8), channel_id=1, replica_groups=mesh['x'=4,'yl'=2,'yh'=2,'z'=8,'core'=2] {'z'}, dimensions={0} | all-to-all | bytes 196608 | tf_op jit(solution)/shard_map/all_to_all | solution.py:433
  75.7 11.4 %all_to_all.32.g_ref = f32[16,24,128]{2,1,0:T(8,128)S(1)} all-to-all(f32[16,24,128]{2,1,0:T(8,128)S(1)} %broadcast_in_dim.10), channel_id=1, replica_groups=mesh['x'=4,'yl'=2,'yh'=2,'z'=8,'core'=2] {'yh','yl','x'}, dimensions={0} | all-to-all | bytes 393216 | tf_op jit(solution)/shard_map/all_to_all | solution.py:433
  87.1 7.7 %solve.1 = (f32[8,12,24,128]{3,2,1,0:T(8,128)}, f32[192,192]{1,0:T(8,128)S(1)}) custom-call(f32[16,24,128]{2,1,0:T(8,128)S(1)} %all_to_all.32.g_ref, f32[8,7,24,128]{3,2,1,0:T(8,128)S(1)} %all-to-all-done.first_ref.r0_ref, f32[8,6,24,128]{3,2,1,0:T(8,128)S(1)} %all-to-all-done.1.second_ref.r1_ref), custom_call_target="tpu_custom_call" | custom-call | tf_op jit(solution)/shard_map/solve/pallas_call | solution.py:386
  94.8 5.5 %all-to-all-start.5 = ((f32[8,12,24,128]{3,2,1,0:T(8,128)}), f32[8,12,24,128]{3,2,1,0:T(8,128)S(1)}, u32[]{:S(2)}, u32[]{:S(2)}) async-start(f32[8,12,24,128]{3,2,1,0:T(8,128)} %get-tuple-element.8), calls=%async_computation.5 | async-start | bytes 2359296 | tf_op jit(solution)/shard_map/all_to_all | solution.py:433
  100.3 0.1 copy.10
  100.5 0.4 fusion
  100.9 1.0 fusion.8
  101.9 11.7 %all-to-all-done.5.t_ref = f32[8,12,24,128]{3,2,1,0:T(8,128)S(1)} async-done(((f32[8,12,24,128]{3,2,1,0:T(8,128)}), f32[8,12,24,128]{3,2,1,0:T(8,128)S(1)}, u32[]{:S(2)}, u32[]{:S(2)}) %all-to-all-start.5) | async-done | bytes 1179680 | tf_op jit(solution)/shard_map/all_to_all | solution.py:433
  113.6 2.0 %unpack.1 = f32[24,96,128]{2,1,0:T(8,128)} custom-call(s32[1]{0:T(128)} %bitcast.turn_ref, f32[8,12,24,128]{3,2,1,0:T(8,128)S(1)} %all-to-all-done.5.t_ref), custom_call_target="tpu_custom_call" | custom-call | tf_op jit(solution)/shard_map/unpack/pallas_call | solution.py:421
  (12 shorter events, 0.1 us)
Async XLA Ops:
  0.6 25.6 %copy-start = (f32[2,16,128]{2,1,0:T(8,128)S(1)}, f32[2,16,128]{2,1,0:T(8,128)}, u32[]{:S(2)}) copy-start(f32[2,16,128]{2,1,0:T(8,128)} %param.3) | copy-start | bytes 49156
  0.7 9.0 %copy-start.1 = (f32[24,3,2,16,128]{4,3,2,1,0:T(8,128)S(1)}, f32[24,3,2,16,128]{4,3,2,1,0:T(8,128)}, u32[]{:S(2)}) copy-start(f32[24,3,2,16,128]{4,3,2,1,0:T(8,128)} %param.2) | copy-start | bytes 3538948
  3.9 16.1 %all-to-all-start = ((f32[8,7,24,128]{3,2,1,0:T(8,128)}), f32[8,7,24,128]{3,2,1,0:T(8,128)S(1)}, u32[]{:S(2)}, u32[]{:S(2)}) async-start(f32[8,7,24,128]{3,2,1,0:T(8,128)} %pack_first.1), calls=%async_computation | async-start | bytes 1376256 | tf_op jit(solution)/shard_map/all_to_all | solution.py:433
  20.0 14.4 %all-to-all-start.1 = ((f32[8,6,24,128]{3,2,1,0:T(8,128)}), f32[8,6,24,128]{3,2,1,0:T(8,128)S(1)}, u32[]{:S(2)}, u32[]{:S(2)}) async-start(f32[8,6,24,128]{3,2,1,0:T(8,128)} %pack_second.1), calls=%async_computation.1 | async-start | bytes 1179648 | tf_op jit(solution)/shard_map/all_to_all | solution.py:433
  25.0 14.9 %collective-permute-start = (f32[8,7,24,128]{3,2,1,0:T(8,128)S(1)}, f32[8,7,24,128]{3,2,1,0:T(8,128)S(1)}, u32[]{:S(2)}, u32[]{:S(2)}) collective-permute-start(f32[8,7,24,128]{3,2,1,0:T(8,128)S(1)} %all-to-all-done.first_ref.r0_ref), channel_id=1, source_target_pairs={{1,0},{2,1},{3,2},{4,3},{5,4},{6,5},{7,6},{8,7},{9,8},{10,9},{11,1... | collective-permute-start | bytes 2064392 | tf_op jit(solution)/shard_map/ppermute | solution.py:463
  58.9 1.3 %collective-permute-start.1 = (f32[24,128]{1,0:T(8,128)S(1)}, f32[24,128]{1,0:T(8,128)S(1)}, u32[]{:S(2)}, u32[]{:S(2)}) collective-permute-start(f32[24,128]{1,0:T(8,128)S(1)} %reduce_sum.18), channel_id=1, source_target_pairs={{0,1},{1,0},{2,3},{3,2},{4,5},{5,4},{6,7},{7,6},{8,9},{9,8},{10,11... | collective-permute-start | bytes 36872 | tf_op jit(solution)/shard_map/ppermute | solution.py:470
  94.8 18.8 %all-to-all-start.5 = ((f32[8,12,24,128]{3,2,1,0:T(8,128)}), f32[8,12,24,128]{3,2,1,0:T(8,128)S(1)}, u32[]{:S(2)}, u32[]{:S(2)}) async-start(f32[8,12,24,128]{3,2,1,0:T(8,128)} %get-tuple-element.8), calls=%async_computation.5 | async-start | bytes 2359296 | tf_op jit(solution)/shard_map/all_to_all | solution.py:433
